TPU v7x, 32 devices: a whole 2x2x4 slice. The times are simulated.
32 devices in a mesh: row: 4 (over x, core), col: 4 (over z), depth: 2 (over y).
Axes of the slice: x: 2, y: 2, z: 4, core: 2. Of those that a mesh axis runs over, the one named last changes fastest.
Arguments:
- normed: bfloat16 [1024, 3072], P(('depth', 'row'), 'col'), may hold values from -6 to 6
- up_weight: bfloat16 [3072, 12288], P('col', 'row'), may hold values from -0.109375 to 0.109375
- down_weight: bfloat16 [12288, 3072], P('row', 'col'), may hold values from -0.0546875 to 0.0546875
- out_grad: bfloat16 [1024, 3072], P(('depth', 'row'), 'col'), may hold values from -6 to 6
Outputs:
- branch_out: bfloat16 [1024, 3072], P(('depth', 'row'), 'col')
- normed_grad: bfloat16 [1024, 3072], P(('depth', 'row'), 'col')
- up_grad: float32 [3072, 12288], P(('col', 'depth'), 'row')
- down_grad: float32 [12288, 3072], P(('row', 'depth'), 'col')
All inputs are finite; a program needn't handle non-finite values.
Results may differ from a plain program's by a relative error of at most 0.029.
Values may be sent and summed in bfloat16 or wider, within the bound.
No kernel may reach another device: no remote copies, remote signals or barrier semaphores. Data moves between devices by JAX's collectives and lax.ppermute only.
A program may use at most 64 MiB of HBM per device.

v0:
```python
import math

import jax
import jax.numpy as jnp
from jax import lax
from jax.sharding import PartitionSpec as P


def gelu_parts(value):
    coeff = math.sqrt(2.0 / math.pi)
    inner = coeff * (value + 0.044715 * value * value * value)
    tangent = jnp.tanh(inner)
    activated = 0.5 * value * (1.0 + tangent)
    slope = 0.5 * (1.0 + tangent) + 0.5 * value * (1.0 - tangent * tangent) * coeff * (
        1.0 + 3.0 * 0.044715 * value * value
    )
    return (activated, slope)


def contract_last(left, right):
    return lax.dot_general(
        left, right, (((1,), (1,)), ((), ())), preferred_element_type=jnp.float32
    )


def contract_first(left, right):
    return lax.dot_general(
        left, right, (((0,), (0,)), ((), ())), preferred_element_type=jnp.float32
    )


def per_device(normed, up_weight, down_weight, out_grad):
    gathered, cotangent = (
        lax.all_gather(normed, "row", axis=0, tiled=True),
        lax.all_gather(out_grad, "row", axis=0, tiled=True),
    )
    up_part = jnp.dot(gathered, up_weight, preferred_element_type=jnp.float32)
    back_part = contract_last(cotangent, down_weight)
    pre_act, back_act = (
        lax.psum(up_part.astype(jnp.bfloat16), "col").astype(jnp.float32),
        lax.psum(back_part.astype(jnp.bfloat16), "col").astype(jnp.float32),
    )
    active_full, slope = gelu_parts(pre_act)
    activated = active_full.astype(jnp.bfloat16)
    pre_grad = (back_act * slope).astype(jnp.bfloat16)
    out_part = jnp.dot(activated, down_weight, preferred_element_type=jnp.float32)
    input_part = contract_last(pre_grad, up_weight)
    branch_sum, input_sum = (
        lax.psum_scatter(
            out_part.astype(jnp.bfloat16), "row", scatter_dimension=0, tiled=True
        ).astype(jnp.float32),
        lax.psum_scatter(
            input_part.astype(jnp.bfloat16), "row", scatter_dimension=0, tiled=True
        ).astype(jnp.float32),
    )
    up_local = contract_first(gathered, pre_grad)
    down_local = contract_first(activated, cotangent)
    up_total, down_total = (
        lax.psum(up_local.astype(jnp.bfloat16), "depth").astype(jnp.float32),
        lax.psum(down_local.astype(jnp.bfloat16), "depth").astype(jnp.float32),
    )
    layers = lax.axis_size("depth")
    depth_index = lax.axis_index("depth")
    up_rows = up_local.shape[0] // layers
    down_rows = down_local.shape[0] // layers
    up_sum = lax.dynamic_slice_in_dim(up_total, depth_index * up_rows, up_rows, 0)
    down_sum = lax.dynamic_slice_in_dim(down_total, depth_index * down_rows, down_rows, 0)
    factor = 1.0 / math.sqrt(gathered.shape[0] * lax.axis_size("depth"))
    return (
        branch_sum.astype(jnp.bfloat16),
        input_sum.astype(jnp.bfloat16),
        up_sum * factor,
        down_sum * factor,
    )


def solution(mesh):
    return jax.shard_map(
        per_device,
        mesh=mesh,
        in_specs=(
            P(("depth", "row"), "col"),
            P("col", "row"),
            P("row", "col"),
            P(("depth", "row"), "col"),
        ),
        out_specs=(
            P(("depth", "row"), "col"),
            P(("depth", "row"), "col"),
            P(("col", "depth"), "row"),
            P(("row", "depth"), "col"),
        ),
        check_vma=False,
    )
```

profile of v0, /device:TPU:0, one launch (start us, length us, event | category | flops | bytes accessed | tf_op | source)
XLA Modules:
  0.0 559.6 jit_solution(9806154549444906535)
XLA Ops:
  7.2 0.0 all-reduce.5.cloned.1.call-start
  7.2 10.3 %all_gather.6 = bf16[512,768]{1,0:T(8,128)(2,1)S(1)} all-gather(bf16[128,768]{1,0:T(8,128)(2,1)} %param.4), channel_id=1, replica_groups=mesh['row'=4,'col'=4,'depth'=2] {'row'}, dimensions={0}, use_global_device_ids=true | all-gather | bytes 983040 | tf_op jit(solution)/shard_map/all_gather | solution.py:34
  17.5 9.0 %all_gather.7 = bf16[512,768]{1,0:T(8,128)(2,1)S(1)} all-gather(bf16[128,768]{1,0:T(8,128)(2,1)} %param.7), channel_id=1, replica_groups=mesh['row'=4,'col'=4,'depth'=2] {'row'}, dimensions={0}, use_global_device_ids=true | all-gather | bytes 983040 | tf_op jit(solution)/shard_map/all_gather | solution.py:35
  26.5 6.6 %convolution_convert_fusion.3 = bf16[512,3072]{1,0:T(8,128)(2,1)} fusion(bf16[512,768]{1,0:T(8,128)(2,1)S(1)} %all_gather.6, bf16[768,3072]{1,0:T(8,128)(2,1)} %param.5), kind=kOutput, calls=%fused_computation.24 | convolution fusion | flops 2417491968 | bytes 8650752 | tf_op jit(solution)/shard_map/dot_general | solution.py:37
  33.1 4.0 convolution_convert_fusion.2
  37.2 0.0 all-reduce.5.cloned.1.call-update
  37.2 0.0 all-reduce.7.cloned.1.call-start
  37.2 224.2 %all-reduce.5.cloned.1.call-done = (bf16[512,3072]{1,0:T(8,128)(2,1)}, bf16[512,3072]{1,0:T(8,128)(2,1)}) async-done(((bf16[512,3072]{1,0:T(8,128)(2,1)}, bf16[512,3072]{1,0:T(8,128)(2,1)}), (bf16[512,3072]{1,0:T(8,128)(2,1)}, bf16[512,3072]{1,0:T(8,128)(2,1)})) %all-reduce.5.cloned.1.call-update) | async-done | bytes 6291472 | tf_op jit(solution)/shard_map/psum | solution.py:40
  261.4 8.1 %convolution_convert_fusion = bf16[3072,768]{1,0:T(8,128)(2,1)} fusion(bf16[512,768]{1,0:T(8,128)(2,1)} %copy-done.5, bf16[512,3072]{1,0:T(8,128)(2,1)} %get-tuple-element.8), kind=kOutput, calls=%fused_computation.18 | convolution fusion | flops 2434007040 | bytes 8650752 | tf_op jit(solution)/shard_map/dot_general | solution.py:27
  269.6 4.4 fusion.7
  274.0 1.6 copy-done.1
  275.7 4.3 fusion.11
  280.0 0.0 all-reduce.7.cloned.1.call-update
  280.0 0.2 reduce-scatter.3.cloned.1.call-start
  280.2 7.2 %convolution_convert_fusion.5 = bf16[512,768]{1,0:T(8,128)(2,1)} fusion(bf16[3072,768]{1,0:T(8,128)(2,1)} %param.6, bf16[512,3072]{1,0:T(8,128)(2,1)S(1)} %copy-done), kind=kOutput, calls=%fused_computation.26 | convolution fusion | flops 2432040960 | bytes 8650752 | tf_op jit(solution)/shard_map/dot_general | solution.py:46
  287.4 0.0 reduce-scatter.3.cloned.1.call-update
  287.5 0.0 reduce-scatter.5.cloned.1.call-start
  287.5 6.8 %convolution_convert_fusion.4 = bf16[512,768]{1,0:T(8,128)(2,1)} fusion(bf16[512,3072]{1,0:T(8,128)(2,1)} %copy-done.1, bf16[768,3072]{1,0:T(8,128)(2,1)} %param.5), kind=kOutput, calls=%fused_computation.25 | convolution fusion | flops 2416312320 | bytes 8650752 | tf_op jit(solution)/shard_map/dot_general | solution.py:21
  294.4 205.9 %all-reduce.7.cloned.1.call-done = (bf16[768,3072]{0,1:T(8,128)(2,1)}, bf16[3072,768]{1,0:T(8,128)(2,1)}) async-done(((bf16[768,3072]{0,1:T(8,128)(2,1)}, bf16[3072,768]{1,0:T(8,128)(2,1)}), (bf16[768,3072]{0,1:T(8,128)(2,1)}, bf16[3072,768]{1,0:T(8,128)(2,1)})) %all-reduce.7.cloned.1.call-update) | async-done | bytes 9437200 | tf_op jit(solution)/shard_map/psum | solution.py:59
  500.3 4.2 convert_multiply_fusion.7
  504.5 6.1 %copy.8 = f32[384,3072]{1,0:T(8,128)} copy(f32[384,3072]{0,1:T(8,128)} %convert_multiply_fusion.7) | data formatting | bytes 9437184
  510.5 4.2 convert_multiply_fusion.6
  514.7 12.0 %reduce-scatter.3.cloned.1.call-done = bf16[128,768]{1,0:T(8,128)(2,1)} async-done(((bf16[512,768]{1,0:T(8,128)(2,1)}), bf16[128,768]{1,0:T(8,128)(2,1)}) %reduce-scatter.3.cloned.1.call-update) | async-done | bytes 196624 | tf_op jit(solution)/shard_map/reduce_scatter | solution.py:49
  526.7 26.4 %reduce-scatter.5.cloned.1.call-done = bf16[128,768]{1,0:T(8,128)(2,1)} async-done(((bf16[512,768]{1,0:T(8,128)(2,1)}), bf16[128,768]{1,0:T(8,128)(2,1)}) %reduce-scatter.5.cloned.1.call-update) | async-done | bytes 196624 | tf_op jit(solution)/shard_map/reduce_scatter | solution.py:52
  (17 shorter events, 0.0 us)
Async XLA Ops:
  7.2 254.3 %all-reduce.5.cloned.1.call-start = ((), (), s32[]{:S(2)}) async-start(), calls=%async_computation.4 | async-start | bytes 12582912 | tf_op jit(solution)/shard_map/psum | solution.py:40
  17.5 9.1 %copy-start.3 = (bf16[512,768]{1,0:T(8,128)(2,1)}, bf16[512,768]{1,0:T(8,128)(2,1)S(1)}, u32[]{:S(2)}) copy-start(bf16[512,768]{1,0:T(8,128)(2,1)S(1)} %all_gather.6) | copy-start | bytes 2359300
  17.5 15.6 %slice-start = ((s8[4718592]{0:T(1024)(128)(4,1)}), s8[4194304]{0:T(1024)(128)(4,1)S(1)}, s32[]{:S(2)}) async-start(s8[4718592]{0:T(1024)(128)(4,1)} %bitcast.12), calls=%async_computation.6 | async-start | bytes 8388608
  26.5 6.6 %copy-start.5 = (bf16[512,768]{1,0:T(8,128)(2,1)}, bf16[512,768]{1,0:T(8,128)(2,1)S(1)}, u32[]{:S(2)}) copy-start(bf16[512,768]{1,0:T(8,128)(2,1)S(1)} %all_gather.7) | copy-start | bytes 2359300
  26.5 6.6 %slice-start.1 = ((s8[4718592]{0:T(1024)(128)(4,1)}), s8[524288]{0:T(1024)(128)(4,1)S(1)}, s32[]{:S(2)}) async-start(s8[4718592]{0:T(1024)(128)(4,1)} %bitcast.12), calls=%async_computation.7 | async-start | bytes 1048576
  37.2 463.1 %all-reduce.7.cloned.1.call-start = ((), (), s32[]{:S(2)}) async-start(), calls=%async_computation.5 | async-start | bytes 18874368 | tf_op jit(solution)/shard_map/psum | solution.py:59
  261.4 8.1 %copy-start = (bf16[512,3072]{1,0:T(8,128)(2,1)S(1)}, bf16[512,3072]{1,0:T(8,128)(2,1)}, u32[]{:S(2)}) copy-start(bf16[512,3072]{1,0:T(8,128)(2,1)} %get-tuple-element.8) | copy-start | bytes 9437188
  261.4 8.1 %copy-start.2 = (bf16[512,3072]{1,0:T(8,128)(2,1)S(1)}, bf16[512,3072]{1,0:T(8,128)(2,1)}, u32[]{:S(2)}) copy-start(bf16[512,3072]{1,0:T(8,128)(2,1)} %get-tuple-element.9) | copy-start | bytes 9437188
  269.6 6.1 %copy-start.4 = (bf16[512,768]{1,0:T(8,128)(2,1)S(1)}, bf16[512,768]{1,0:T(8,128)(2,1)}, u32[]{:S(2)}) copy-start(bf16[512,768]{1,0:T(8,128)(2,1)} %copy-done.3) | copy-start | bytes 2359300
  274.0 1.7 copy-start.1
  280.0 246.7 %reduce-scatter.3.cloned.1.call-start = ((), (), s32[]{:S(2)}) async-start(), calls=%async_computation.2 | async-start | bytes 983040 | tf_op jit(solution)/shard_map/reduce_scatter | solution.py:49
  287.5 265.6 %reduce-scatter.5.cloned.1.call-start = ((), (), s32[]{:S(2)}) async-start(), calls=%async_computation.3 | async-start | bytes 983040 | tf_op jit(solution)/shard_map/reduce_scatter | solution.py:52
Sparse Core Ops, SparseCore 0:
  37.3 224.0 all-reduce.4
  280.1 220.1 all-reduce.6
  503.4 23.2 reduce-scatter.2
  529.8 23.2 reduce-scatter.4
where the time goes:
time: 560 us
  waiting for transfers between devices  469 us (84%)
  matrix products  37.1 us (7%)
  blocking collectives  19.3 us (3%)
  between operations  13.8 us (2%)
  other arithmetic  12.8 us (2%)
  local copies, waits for them, and re-layouts  7.73 us (1%)
    psum x1, waiting for transfers between devices, per_device(): lax.psum(up_part.astype(jnp.bfloat16), 'col').astype(jnp.float32)  224 us
    psum x1, waiting for transfers between devices, per_device(): lax.psum(up_local.astype(jnp.bfloat16), 'depth').astype(jnp.float32)  206 us
    reduce_scatter x1, waiting for transfers between devices, per_device(): lax.psum_scatter(input_part.astype(jnp.bfloat16), 'row', scatter_dimensio...  26.4 us
    dot_general x2, matrix products, contract_first(): lax.dot_general(left, right, (((0,), (0,)), ((), ())), preferred_element_...  12.4 us
    reduce_scatter x1, waiting for transfers between devices, per_device(): lax.psum_scatter(out_part.astype(jnp.bfloat16), 'row', scatter_dimension=...  12 us
  transfers between devices with their start and end apart: 4, of which 4 were waited for; matrix products, arithmetic and copies ran while one was open for 5% of the time, Pallas kernels for 0%

commit v1 on v0

v1 whole, which is shorter than its diff:
```python
import math

import jax
import jax.numpy as jnp
from jax import lax
from jax.experimental import pallas as pl
from jax.experimental.pallas import tpu as pltpu
from jax.sharding import PartitionSpec as P

F_PHASES = 3
STREAMS = 2
ROWS = 32


def gelu_parts(value):
    coeff = math.sqrt(2.0 / math.pi)
    inner = coeff * (value + 0.044715 * value * value * value)
    tangent = jnp.tanh(inner)
    activated = 0.5 * value * (1.0 + tangent)
    slope = 0.5 * (1.0 + tangent) + 0.5 * value * (1.0 - tangent * tangent) * coeff * (
        1.0 + 3.0 * 0.044715 * value * value
    )
    return (activated, slope)


def dot(left, right, left_dim, right_dim):
    return lax.dot_general(
        left, right, (((left_dim,), (right_dim,)), ((), ())), preferred_element_type=jnp.float32
    )


def to_bf16(value):
    return value.astype(jnp.bfloat16)


def to_f32(value):
    return value.astype(jnp.float32)


def cut_at(array, start, size, dim):
    starts, sizes = [0] * array.ndim, list(array.shape)
    starts[dim], sizes[dim] = start, size
    return lax.dynamic_slice(array, starts, sizes, allow_negative_indices=False)


def put_at(array, part, start, dim):
    starts = [0] * array.ndim
    starts[dim] = start
    return lax.dynamic_update_slice(array, part, starts, allow_negative_indices=False)


def swap(value, axis, mask):
    size = lax.axis_size(axis)
    return lax.ppermute(value, axis, [(i, i ^ mask) for i in range(size)])


def bits(size):
    return [1 << b for b in range(size.bit_length() - 1)]


def by_rows(count, body):
    def step(index, carry):
        body(pl.ds(pl.multiple_of(index * ROWS, ROWS), ROWS))
        return carry

    lax.fori_loop(0, count // ROWS, step, 0)


def bf16_array(*shape):
    return jax.ShapeDtypeStruct(shape, jnp.bfloat16)


def f32_array(*shape):
    return jax.ShapeDtypeStruct(shape, jnp.float32)


NO_COST = pl.CostEstimate(flops=1, bytes_accessed=1, transcendentals=0)
IN_VMEM = pl.BlockSpec(memory_space=pltpu.VMEM)
IN_SMEM = pl.BlockSpec(memory_space=pltpu.SMEM)


def local_kernel(body, out_shapes, scalar, operands, limit=8):
    scalars = [] if scalar is None else [scalar]
    return pl.pallas_call(
        body,
        out_shape=out_shapes,
        in_specs=[IN_SMEM] * len(scalars) + [IN_VMEM] * len(operands),
        out_specs=[IN_VMEM] * len(out_shapes),
        compiler_params=pltpu.CompilerParams(vmem_limit_bytes=limit * 2**20),
        cost_estimate=NO_COST,
    )(*scalars, *operands)


def spans(blocks):
    result, start = [], 0
    for block in blocks:
        result.append((block, start, start + block.shape[1]))
        start += block.shape[1]
    return result


def partials(start, blocks, up, down, half):
    count = sum(block.shape[1] for block in blocks)

    def body(*refs):
        *block_refs, up_ref, down_ref, out_ref = refs
        for k in range(2):
            at = slice(start + k * half, start + (k + 1) * half)
            for block, first, end in spans(block_refs):
                out_ref[k, 0, first:end] = to_bf16(dot(block[0], up_ref[:, at], 1, 0))
                out_ref[k, 1, first:end] = to_bf16(dot(block[1], down_ref[at, :], 1, 1))

    if half % 128:
        part = jnp.concatenate(blocks, axis=1)
        cut = [slice(start + k * half, start + (k + 1) * half) for k in range(2)]
        return to_bf16(
            jnp.stack(
                [
                    jnp.stack([dot(part[0], up[:, at], 1, 0), dot(part[1], down[at], 1, 1)])
                    for at in cut
                ]
            )
        )
    return local_kernel(body, [bf16_array(2, 2, count, half)], None, [*blocks, up, down])[0]


COPIES = 4


def load(column, up_weight, down_weight, start, size, limit):
    features = up_weight.shape[0]
    rows, part = features // COPIES, size // COPIES

    def body(column_ref, up_hbm, down_hbm, up_ref, down_ref, done):
        first = pl.multiple_of(column_ref[0] + start, size)
        copies = []
        for k in range(COPIES):
            at = pl.ds(k * rows, rows)
            copies.append((up_hbm.at[at, pl.ds(first, size)], up_ref.at[at, :]))
            there = pl.ds(pl.multiple_of(first + k * part, part), part)
            copies.append((down_hbm.at[there, :], down_ref.at[pl.ds(k * part, part), :]))
        copies = [
            pltpu.make_async_copy(source, target, done.at[k])
            for k, (source, target) in enumerate(copies)
        ]
        for copy in copies:
            copy.start()
        for copy in copies:
            copy.wait()

    in_place = pl.BlockSpec(memory_space=pl.ANY)
    return pl.pallas_call(
        body,
        out_shape=[bf16_array(features, size), bf16_array(size, features)],
        in_specs=[IN_SMEM, in_place, in_place],
        out_specs=[IN_VMEM] * 2,
        scratch_shapes=[pltpu.SemaphoreType.DMA((2 * COPIES,))],
        compiler_params=pltpu.CompilerParams(vmem_limit_bytes=limit * 2**20),
        cost_estimate=NO_COST,
    )(column, up_weight, down_weight)


def outputs_of(start, done, up, down, so_far, sizes):
    half, features = done.shape[3], up.shape[0]

    def total(done, up, down, before):
        value = list(before)
        for k in range(2):
            at = slice(start + k * half, start + (k + 1) * half)
            value[0] = value[0] + dot(done[k, 0], down[at, :], 1, 0)
            value[1] = value[1] + dot(done[k, 1], up[:, at], 1, 1)
        return value

    def body(done_ref, up_ref, down_ref, *refs):
        outs = refs[-len(sizes) :]
        befores = refs[: -len(sizes)]
        for kind, value in enumerate(total(done_ref, up_ref, down_ref, (0.0, 0.0))):
            first = 0
            for place, size in enumerate(sizes):
                part = value[first : first + size]
                if befores:
                    part = part + to_f32(befores[place][kind])
                outs[place][kind] = to_bf16(part)
                first += size

    if half % 128:
        before = (0.0, 0.0)
        if so_far:
            before = to_f32(jnp.concatenate(so_far, axis=1))
        value = to_bf16(jnp.stack(total(done, up, down, before)))
        return jnp.split(value, [sum(sizes[:k]) for k in range(1, len(sizes))], axis=1)
    shapes = [bf16_array(2, size, features) for size in sizes]
    return local_kernel(body, shapes, None, [done, up, down, *so_far])


def sum_of(blocks):
    if len(blocks) == 1:
        return blocks[0]

    def body(*refs):
        def rows(at):
            for kind in range(2):
                total = to_f32(refs[0][kind, at, :])
                for ref in refs[1:-1]:
                    total = total + to_f32(ref[kind, at, :])
                refs[-1][kind, at, :] = to_bf16(total)

        by_rows(blocks[0].shape[1], rows)

    return local_kernel(body, [bf16_array(*blocks[0].shape)], None, blocks)[0]


def gradient(kind, so_far, done, parts):
    half, features = done[0].shape[3], parts[0][0].shape[2]
    pairs = len(done)
    if half % 128:
        total = 0.0 if so_far is None else so_far
        for value, blocks in zip(done, parts):
            both = jnp.concatenate([value[0, kind], value[1, kind]], axis=-1)
            block = jnp.concatenate(blocks, axis=1)[1 - kind]
            total = total + (dot(block, both, 0, 0) if kind else dot(both, block, 0, 0))
        return total

    def body(*refs):
        done_refs, block_refs, out_ref = refs[:pairs], list(refs[pairs:-1]), refs[-1]
        part_refs = [[block_refs.pop(0) for _ in blocks] for blocks in parts]
        for k in range(2):
            at = slice(k * half, (k + 1) * half)
            total = 0.0
            if so_far is not None:
                total = block_refs[0][:, at] if kind else block_refs[0][at, :]
            for done_ref, blocks in zip(done_refs, part_refs):
                for block, first, end in spans(blocks):
                    value = done_ref[k, kind, first:end]
                    if kind:
                        total = total + dot(block[0], value, 0, 0)
                    else:
                        total = total + dot(value, block[1], 0, 0)
            if kind:
                out_ref[:, at] = total
            else:
                out_ref[at, :] = total

    shape = f32_array(features, 2 * half) if kind else f32_array(2 * half, features)
    operands = [*done, *(block for blocks in parts for block in blocks)]
    operands += [] if so_far is None else [so_far]
    return local_kernel(body, [shape], None, operands, 12)[0]


def up_rows(row, size, sums, done, parts, kind):
    half = sums.shape[1] // 2
    if half % 128:
        total = cut_at(sums, row[0], size, 0)
        for value, blocks in zip(done, parts):
            tokens = cut_at(jnp.concatenate(blocks, axis=1)[0], row[0], size, 1)
            total = total + dot(tokens, jnp.concatenate([value[0, 1], value[1, 1]], axis=-1), 0, 0)
        return total.astype(kind)

    def body(row_ref, sums_ref, *refs):
        at = pl.ds(pl.multiple_of(row_ref[0], size), size)
        out_ref, done_refs = refs[-1], refs[: len(done)]
        block_refs = list(refs[len(done) : -1])
        part_refs = [[block_refs.pop(0) for _ in blocks] for blocks in parts]
        for k in range(2):
            columns = slice(k * half, (k + 1) * half)
            total = sums_ref[at, columns]
            for done_ref, blocks in zip(done_refs, part_refs):
                for block, first, end in spans(blocks):
                    total = total + dot(block[0, :, at], done_ref[k, 1, first:end], 0, 0)
            out_ref[:, columns] = total.astype(kind)

    operands = [sums, *done, *(block for blocks in parts for block in blocks)]
    shape = jax.ShapeDtypeStruct((size, 2 * half), kind)
    return local_kernel(body, [shape], row, operands)[0]


def all_of_up(y, factor, blocks, size, width):
    phases, f_width = len(blocks[0]), blocks[0][0].shape[1]
    flat = [block for row in blocks for block in row]
    if f_width % 128 or size % 128:
        result = jnp.zeros((size, width * len(blocks)), jnp.float32)
        for mask, row in enumerate(blocks):
            for phase, block in enumerate(row):
                start = (y[0] ^ mask) * width + phase * f_width
                result = put_at(result, to_f32(block) * factor, start, 1)
        return result

    def put(base, chosen):
        def place_of(step, y):
            result = 0
            for index, (mask, phase) in enumerate(chosen):
                result = jnp.where(step == index, (y[0] ^ mask) * phases + phase, result)
            return result

        def body(y_ref, *refs):
            for index in range(len(chosen)):

                @pl.when(pl.program_id(0) == index)
                def _(ref=refs[index]):
                    refs[-1][...] = to_f32(ref[...]) * factor

        arrays = [blocks[mask][phase] for mask, phase in chosen]
        return pl.pallas_call(
            body,
            out_shape=f32_array(size, width * len(blocks)),
            grid_spec=pltpu.PrefetchScalarGridSpec(
                num_scalar_prefetch=1,
                grid=(len(chosen),),
                in_specs=[IN_VMEM] * len(arrays)
                + [pl.BlockSpec(memory_space=pl.ANY)] * (base is not None),
                out_specs=pl.BlockSpec((size, f_width), lambda step, y: (0, place_of(step, y))),
            ),
            input_output_aliases={} if base is None else {1 + len(arrays): 0},
            compiler_params=pltpu.CompilerParams(vmem_limit_bytes=8 * 2**20),
            cost_estimate=NO_COST,
        )(y, *arrays, *([] if base is None else [base]))

    every = [(mask, phase) for mask in range(len(blocks)) for phase in range(phases)]
    late = [(mask, phase) for mask, phase in every if mask and phase == phases - 1]
    return put(put(None, [pair for pair in every if pair not in late]), late)


def all_of_down(factor, sums, done, parts):
    f_width, features = sums[-1].shape
    half = f_width // 2
    if half % 128:
        total = sums[-1]
        for value, blocks in zip(done, parts):
            both = jnp.concatenate([value[0, 0], value[1, 0]], axis=-1)
            total = total + dot(both, jnp.concatenate(blocks, axis=1)[1], 0, 0)
        return jnp.concatenate([*sums[:-1], total], axis=0) * factor
    steps = 2 * len(sums)

    def body(*refs):
        step, out_ref = pl.program_id(0), refs[-1]
        sum_refs, done_refs = refs[: len(sums)], refs[len(sums) : len(sums) + len(done)]
        block_refs = list(refs[len(sums) + len(done) : -1])
        part_refs = [[block_refs.pop(0) for _ in blocks] for blocks in parts]
        for index in range(steps):

            @pl.when(step == index)
            def _(index=index):
                phase, k = divmod(index, 2)
                total = sum_refs[phase][k * half : (k + 1) * half, :]
                if phase == len(sums) - 1:
                    for done_ref, blocks in zip(done_refs, part_refs):
                        for block, first, end in spans(blocks):
                            total = total + dot(done_ref[k, 0, first:end], block[1], 0, 0)
                out_ref[...] = total * factor

    operands = [*sums, *done, *(block for blocks in parts for block in blocks)]
    return pl.pallas_call(
        body,
        out_shape=f32_array(f_width * len(sums), features),
        grid=(steps,),
        in_specs=[IN_VMEM] * len(operands),
        out_specs=pl.BlockSpec((half, features), lambda step: (step, 0)),
        compiler_params=pltpu.CompilerParams(vmem_limit_bytes=12 * 2**20),
        cost_estimate=NO_COST,
    )(*operands)


def add_inward(place, piece, outer, middle):
    _, _, count, half = piece.shape
    back = 0 if middle is None else middle.shape[1]

    def body(place_ref, piece, outer, *refs):
        place = place_ref[0]
        middle = refs[0] if back else None
        out, inward = refs[-2:]

        def copy(source, size):
            def rows(at):
                out[:, at, :] = source[:, at, :]

            by_rows(size, rows)

        def add(other):
            def rows(at):
                inward[:, at, :] = to_bf16(to_f32(other[:, at, :]) + to_f32(outer[:, at, :]))

            by_rows(count, rows)

        pl.when(place == 0)(lambda: copy(piece.at[0], count))
        pl.when(place == 3)(lambda: copy(piece.at[1], count))
        pl.when(place == 1)(lambda: add(piece.at[1]))
        pl.when(place == 2)(lambda: add(piece.at[0]))
        if back:
            pl.when((place == 1) | (place == 2))(lambda: copy(middle, back))

    shapes = [bf16_array(2, max(count, back), half), bf16_array(2, count, half)]
    operands = [piece, outer] + ([middle] if back else [])
    return local_kernel(body, shapes, place, operands)


def turn_outward(place, piece, outer, middle, following):
    _, _, count, half = piece.shape
    ahead = 0 if following is None else following.shape[2]

    def body(place_ref, piece, outer, middle, *refs):
        place = place_ref[0]
        out, result = refs[-2:]

        def copy(source):
            def rows(at):
                out[:, at, :] = source[:, at, :]

            by_rows(ahead, rows)

        def activate(own):
            def rows(at):
                total = [
                    to_f32(own[k, at, :]) + to_f32(outer[k, at, :]) + to_f32(middle[k, at, :])
                    for k in range(2)
                ]
                active, slope = gelu_parts(total[0])
                for k, value in enumerate((to_bf16(active), to_bf16(total[1] * slope))):
                    result[k, at, :] = value
                    out[k, at, :] = value

            by_rows(count, rows)

        if ahead:
            pl.when(place == 0)(lambda: copy(refs[0].at[1]))
            pl.when(place == 3)(lambda: copy(refs[0].at[0]))
        pl.when(place == 1)(lambda: activate(piece.at[0]))
        pl.when(place == 2)(lambda: activate(piece.at[1]))

    shapes = [bf16_array(2, max(count, ahead), half), bf16_array(2, count, half)]
    operands = [piece, outer, middle] + ([following] if ahead else [])
    return local_kernel(body, shapes, place, operands)


def collect(place, before, outer, outer_2, middle):
    _, count, half = before.shape

    def body(place_ref, before, outer, outer_2, middle, done):
        for index, (low, high) in enumerate(
            [(outer, outer_2), (before, middle), (middle, before), (outer_2, outer)]
        ):

            @pl.when(place_ref[0] == index)
            def _(low=low, high=high):
                def rows(at):
                    done[0, :, at, :] = low[:, at, :]
                    done[1, :, at, :] = high[:, at, :]

                by_rows(count, rows)

    operands = [before, outer, outer_2, middle]
    return local_kernel(body, [bf16_array(2, 2, count, half)], place, operands)[0]


def start_out(place, piece):
    _, _, count, half = piece.shape

    def body(place_ref, piece, out):
        def copy(k):
            def rows(at):
                out[:, at, :] = piece[k, :, at, :]

            by_rows(count, rows)

        pl.when(place_ref[0] == 0)(lambda: copy(1))
        pl.when(place_ref[0] > 0)(lambda: copy(0))

    return local_kernel(body, [bf16_array(2, count, half)], place, [piece])[0]


def line(place, pieces, take, finish):
    pieces = list(pieces)
    piece = take(pieces[0])
    out, before, last = start_out(place, piece), None, None
    for index, upcoming in zip(pieces + [None], pieces[1:] + [None, None]):
        outer, middle = yield out, before
        if index is None:
            outer_2, middle_2 = yield middle, None
        else:
            outer_2, middle_2 = yield add_inward(place, piece, outer, middle)
        if before is not None:
            finish(last, collect(place, before, outer, outer_2, middle))
        if index is not None:
            following = None if upcoming is None else take(upcoming)
            out, before = turn_outward(place, piece, outer_2, middle_2, following)
            piece, last = following, index


def line_swaps(outer, middle):
    arrived = [None, None]
    if outer is not None:
        arrived[0] = lax.ppermute(outer, "col", [(0, 1), (1, 0), (2, 3), (3, 2)])
    if middle is not None:
        arrived[1] = lax.ppermute(middle, "col", [(1, 2), (2, 1)])
    return tuple(arrived)


def per_device(normed, up_weight, down_weight, out_grad):
    n_row, n_col, n_depth = (lax.axis_size(axis) for axis in ("row", "col", "depth"))
    assert n_col == 4
    z, y = lax.axis_index("col"), lax.axis_index("depth")
    width = up_weight.shape[1] // n_depth
    phases = F_PHASES if width % (F_PHASES * 256) == 0 else 1
    f_width = width // phases
    half = f_width // 2
    d_rows = normed.shape[1] // n_depth
    factor = 1.0 / math.sqrt(normed.shape[0] * n_row * n_depth)

    scalars = (
        z.reshape(1),
        y.reshape(1),
        (y * width).reshape(1),
        [((y ^ mask) * d_rows).reshape(1) for mask in range(n_depth)],
    )
    scalars, normed, out_grad, up_weight, down_weight = lax.optimization_barrier(
        (scalars, normed, out_grad, up_weight, down_weight)
    )
    place, layer, first_column, row_at = scalars

    stages = [("depth", mask) for mask in bits(n_depth)]
    stages += [("row", mask) for mask in reversed(bits(n_row))]
    own = normed.shape[0]
    core = stages.pop()
    unit = max(own, (own << len(stages)) // 4)
    early_start = own == unit and half % 128 == 0 and phases == F_PHASES and len(stages) == 2
    early_start = early_start and stages[0][0] == "depth"
    lower = [jnp.stack([normed, out_grad])]
    weights = []
    if early_start:
        upper = [swap(lower[0], *core)]
        weights.append(load(first_column, up_weight, down_weight, 0, f_width, 57))
    else:
        for axis, mask in stages:
            lower += [swap(block, axis, mask) for block in lower]
            if sum(block.shape[1] for block in lower) <= unit:
                lower = [jnp.concatenate(lower, axis=1)]
        upper = [swap(block, *core) for block in lower]
        up = cut_at(up_weight, first_column[0], width, 1)
        down = cut_at(down_weight, first_column[0], width, 0)
        for phase in range(phases):
            at = slice(phase * f_width, (phase + 1) * f_width)
            weights.append((up[:, at], down[at]))

    def gather(slot, value):
        if not early_start or slot not in (2, 4, 5, 7):
            return value
        k = (2, 4, 5, 7).index(slot)
        value, lower[k] = lax.optimization_barrier((value, lower[k]))
        if k == 0:
            lower.extend([swap(lower[0], *stages[0]), swap(lower[0], *stages[1])])
        else:
            upper.append(swap(lower[k], *core))
        if k == 1:
            lower.append(swap(lower[1], *stages[1]))
        return value

    if early_start:
        pieces = [(k, True, True) for k in range(4)]
        order = [(0, 0), (1, 0), (0, 1), (0, 2), (0, 3), (1, 3), (1, 1), (1, 2)]
        order += [(2, 3), (2, 1), (2, 2), (2, 0)]
        order = [(phase,) + pieces[k] for phase, k in order]
    else:
        pieces = [(0, True, False), (0, False, True)] + [(k, True, True) for k in range(1, 4)]
        order = [(0,) + piece for piece in pieces]
        for phase in range(1, phases):
            order += [(phase,) + piece for piece in reversed(pieces)]

    def tokens_of(piece):
        k, has_lower, has_upper = piece
        return [lower[k]] * has_lower + [upper[k]] * has_upper

    def take(index):
        phase, piece = order[index][0], order[index][1:]
        if len(weights) == phase:
            start = phase * f_width
            weights.append(load(first_column, up_weight, down_weight, start, f_width, 8))
        return partials(0, tokens_of(piece), *weights[phase], half)

    outputs, arrived, due = {}, [], []
    seen, kept = [0] * phases, [[] for _ in range(phases)]
    ups, downs, up_blocks = [None] * phases, [None] * phases, [[None] * phases for _ in range(n_depth)]
    slot = 0

    def want(holder, key, slots):
        due.append((slot + slots, holder, key))

    def settle(value, last):
        ready = [(holder, key) for limit, holder, key in due if limit <= last]
        due[:] = [entry for entry in due if entry[0] > last]
        value, arrays = lax.optimization_barrier((value, [holder[key] for holder, key in ready]))
        for (holder, key), array in zip(ready, arrays):
            holder[key] = array
        return value

    def bring(start, total, stage, slots):
        arrived.append([start, swap(total, *stage)])
        want(arrived[-1], 1, slots)

    def send(piece, local):
        k, has_lower, has_upper = piece
        if has_upper:
            bring(k * unit, local[-1], core, 3)
        if not has_lower:
            return
        first = k * unit
        places = [(first, unit)]
        if k == 0:
            small = [own << s for s in range(len(stages)) if own << s < unit]
            places = [(size, size) for size in reversed(small)] + [(0, own)]
        for at, size in places:
            blocks = [local[0][:, at - first : at - first + size]]
            for start, block in arrived:
                if start <= at and at + size <= start + block.shape[1]:
                    blocks.append(block[:, at - start : at - start + size])
            total = None if at == 0 and early_start else sum_of(blocks)
            if at == 0 and early_start:
                outputs["local"] = blocks[0]
            elif at == 0:
                outputs["own"] = total
            else:
                stage = (at // own).bit_length() - 1
                bring(at - (own << stage), total, stages[stage], 6)

    def finish(index, done):
        phase, piece = order[index][0], order[index][1:]
        blocks = tokens_of(piece)
        is_last = phase == phases - 1

        seen[phase] += 1
        kept[phase].append((done, blocks))
        is_end = seen[phase] == len(pieces)
        is_rest = is_last and index >= len(order) - 2
        count = sum(block.shape[1] for _, held in kept[phase] for block in held)
        if not is_rest and (count >= 2 * unit or is_end):
            ups[phase] = gradient(1, ups[phase], *zip(*kept[phase]))
            downs[phase] = gradient(0, downs[phase], *zip(*kept[phase]))
            want(ups, phase, 4)
            want(downs, phase, 6)
            kept[phase].clear()
        if is_end:
            rest = list(zip(*kept[phase])) or [[], []]
            for mask in reversed(range(n_depth)):
                kind = jnp.bfloat16 if mask else jnp.float32
                rows = up_rows(row_at[mask], d_rows, ups[phase], *rest, kind)
                up_blocks[mask][phase] = swap(rows, "depth", mask) if mask else rows
                if mask and not is_last:
                    want(up_blocks[mask], phase, 8)
            if is_last:
                outputs["down"] = all_of_down(factor, downs, *rest)

        sizes = [block.shape[1] for block in blocks]
        outputs[piece] = list(
            outputs_of(0, done, *weights[phase], outputs.get(piece, []), sizes)
        )
        if is_last:
            send(piece, outputs[piece])
        else:
            for part in range(len(sizes)):
                want(outputs[piece], part, 5)

    streams = [
        line(place, range(stream, len(order), STREAMS), take, finish) for stream in range(STREAMS)
    ]
    came = [None] * STREAMS
    payload = None
    while any(streams):
        for which, stream in enumerate(streams):
            if stream is None:
                continue
            slot += 1
            if came[which] is not None:
                came[which] = gather(slot, settle(came[which], slot))
                came[which], _ = lax.optimization_barrier((came[which], payload))
            elif slot == 2:
                payload = gather(slot, payload)
            try:
                payload = lax.optimization_barrier(stream.send(came[which]))
                came[which] = line_swaps(*payload)
            except StopIteration:
                streams[which] = None
    if early_start:
        blocks = [block for start, block in arrived if start == 0]
        outputs["own"] = sum_of([outputs["local"]] + blocks)
    up_grad = all_of_up(layer, factor, up_blocks, d_rows, width)
    return (outputs["own"][0], outputs["own"][1], up_grad, outputs["down"])


def solution(mesh):
    return jax.shard_map(
        per_device,
        mesh=mesh,
        in_specs=(
            P(("depth", "row"), "col"),
            P("col", "row"),
            P("row", "col"),
            P(("depth", "row"), "col"),
        ),
        out_specs=(
            P(("depth", "row"), "col"),
            P(("depth", "row"), "col"),
            P(("col", "depth"), "row"),
            P(("row", "depth"), "col"),
        ),
        check_vma=False,
    )
```

time: 560 us -> 206 us (0.37)
  waiting for transfers between devices: 469 us -> 31.8 us
  starting transfers between devices: 0.35 us -> 118 us
  Pallas kernels: 0 us -> 47 us
  matrix products: 37.1 us -> 0 us
  blocking collectives: 19.3 us -> 0 us
  between operations: 13.8 us -> 2.01 us
  other arithmetic: 12.8 us -> 1.21 us
    psum x2 -> x0, waiting for transfers between devices: 430 us -> none  [the longest x1 224 us: per_device(): lax.psum(up_part.astype(jnp.bfloat16), 'col').astype(jnp.float32)]
    ppermute x0 -> x69, starting transfers between devices: none -> 118 us  [the longest x28 89.8 us: line_swaps(): arrived[0] = lax.ppermute(outer, 'col', [(0, 1), (1, 0), (2, 3), (3, 2)])]
    pallas_call x0 -> x98, Pallas kernels: none -> 47 us  [the longest x92 34.1 us: local_kernel(): pl.pallas_call(body, out_shape=out_shapes, in_specs=[IN_SMEM] * len(scala...]
    reduce_scatter x2 -> x0, waiting for transfers between devices: 38.4 us -> none  [the longest x1 26.4 us: per_device(): lax.psum_scatter(input_part.astype(jnp.bfloat16), 'row', scatter_dimensio...]
    dot_general x6 -> x0, matrix products: 37.1 us -> none  [the longest x2 12.4 us: contract_first(): lax.dot_general(left, right, (((0,), (0,)), ((), ())), preferred_element_...]
    ppermute x0 -> x69, waiting for transfers between devices: none -> 31.8 us  [the longest x28 23.6 us: line_swaps(): arrived[0] = lax.ppermute(outer, 'col', [(0, 1), (1, 0), (2, 3), (3, 2)])]
    all_gather x2 -> x0, blocking collectives: 19.3 us -> none  [the longest x1 10.3 us: per_device(): lax.all_gather(normed, 'row', axis=0, tiled=True)]
    mul x2 -> x0, other arithmetic: 8.37 us -> none  [the longest x1 4.22 us: per_device(): down_sum * factor]
  transfers between devices with their start and end apart: 4 -> 69, of which waited for: 4 -> 12; matrix products, arithmetic and copies ran while one was open for 5% -> 0% of each run, Pallas kernels for 0% -> 22%
where the time goes in v1:
time: 206 us; the launch traced here: 205 us
  starting transfers between devices  118 us (57%)
  Pallas kernels  47 us (23%)
  waiting for transfers between devices  31.8 us (15%)
  local copies, waits for them, and re-layouts  5.41 us (3%)
    ppermute x28, starting transfers between devices, line_swaps(): arrived[0] = lax.ppermute(outer, 'col', [(0, 1), (1, 0), (2, 3), (3, 2)])  89.8 us
    pallas_call x92, Pallas kernels, local_kernel(): pl.pallas_call(body, out_shape=out_shapes, in_specs=[IN_SMEM] * len(scala...  34.1 us
    ppermute x28, waiting for transfers between devices, line_swaps(): arrived[0] = lax.ppermute(outer, 'col', [(0, 1), (1, 0), (2, 3), (3, 2)])  23.6 us
    ppermute x24, starting transfers between devices, line_swaps(): arrived[1] = lax.ppermute(middle, 'col', [(1, 2), (2, 1)])  16.2 us
    ppermute x17, starting transfers between devices, swap(): return lax.ppermute(value, axis, [(i, i ^ mask) for i in range(size)])  11.7 us
    ppermute x17, waiting for transfers between devices, swap(): return lax.ppermute(value, axis, [(i, i ^ mask) for i in range(size)])  8.1 us
    pallas_call x3, Pallas kernels, load(): pl.pallas_call(body, out_shape=[bf16_array(features, size), bf16_array(si...  5.09 us
    unnamed x18, local copies, waits for them, and re-layouts  4.64 us
  transfers between devices with their start and end apart: 69, of which 12 were waited for; matrix products, arithmetic and copies ran while one was open for 0% of the time, Pallas kernels for 22%

profile of v1, /device:TPU:0, one launch (start us, length us, event | category | flops | bytes accessed | tf_op | source)
XLA Modules:
  0.0 205.0 jit_solution(12812144401556843392)
XLA Ops:
  22.5 4.0 %collective-permute-done.1.outer = bf16[2,256,256]{2,1,0:T(8,128)(2,1)S(1)} collective-permute-done((bf16[2,256,256]{2,1,0:T(8,128)(2,1)S(1)}, bf16[2,256,256]{2,1,0:T(8,128)(2,1)S(1)}, u32[]{:S(2)}, u32[]{:S(2)}) %collective-permute-start.1) | collective-permute-done | bytes 262176 | tf_op jit(solution)/shard_map/ppermute | solution.py:491
  27.5 4.4 %collective-permute-done.5.outer = bf16[2,256,256]{2,1,0:T(8,128)(2,1)S(1)} collective-permute-done((bf16[2,256,256]{2,1,0:T(8,128)(2,1)S(1)}, bf16[2,256,256]{2,1,0:T(8,128)(2,1)S(1)}, u32[]{:S(2)}, u32[]{:S(2)}) %collective-permute-start.5) | collective-permute-done | bytes 262176 | tf_op jit(solution)/shard_map/ppermute | solution.py:491
  35.1 4.7 %collective-permute-start.9 = (bf16[2,256,256]{2,1,0:T(8,128)(2,1)S(1)}, bf16[2,256,256]{2,1,0:T(8,128)(2,1)S(1)}, u32[]{:S(2)}, u32[]{:S(2)}) collective-permute-start(bf16[2,256,256]{2,1,0:T(8,128)(2,1)S(1)} %get-tuple-element.270), channel_id=1, source_target_pairs={{0,2},{2,0},{4,6},{6,4},{1,3},{3,1},{5,7},{7,5},{8,10},{10,8},{12,... | collective-permute-start | bytes 786440 | tf_op jit(solution)/shard_map/ppermute | solution.py:491
  41.4 5.4 %collective-permute-start.15 = (bf16[2,256,256]{2,1,0:T(8,128)(2,1)S(1)}, bf16[2,256,256]{2,1,0:T(8,128)(2,1)S(1)}, u32[]{:S(2)}, u32[]{:S(2)}) collective-permute-start(bf16[2,256,256]{2,1,0:T(8,128)(2,1)S(1)} %get-tuple-element.279), channel_id=1, source_target_pairs={{0,2},{2,0},{4,6},{6,4},{1,3},{3,1},{5,7},{7,5},{8,10},{10,8},{12,... | collective-permute-start | bytes 786440 | tf_op jit(solution)/shard_map/ppermute | solution.py:491
  47.7 3.5 %collective-permute-start.19 = (bf16[2,256,256]{2,1,0:T(8,128)(2,1)S(1)}, bf16[2,256,256]{2,1,0:T(8,128)(2,1)S(1)}, u32[]{:S(2)}, u32[]{:S(2)}) collective-permute-start(bf16[2,256,256]{2,1,0:T(8,128)(2,1)S(1)} %get-tuple-element.287), channel_id=1, source_target_pairs={{0,2},{2,0},{4,6},{6,4},{1,3},{3,1},{5,7},{7,5},{8,10},{10,8},{12,... | collective-permute-start | bytes 786440 | tf_op jit(solution)/shard_map/ppermute | solution.py:491
  52.5 4.0 %collective-permute-start.17 = (bf16[2,256,256]{2,1,0:T(8,128)(2,1)S(1)}, bf16[2,256,256]{2,1,0:T(8,128)(2,1)S(1)}, u32[]{:S(2)}, u32[]{:S(2)}) collective-permute-start(bf16[2,256,256]{2,1,0:T(8,128)(2,1)S(1)} %get-tuple-element.291), channel_id=1, source_target_pairs={{0,2},{2,0},{4,6},{6,4},{1,3},{3,1},{5,7},{7,5},{8,10},{10,8},{12,... | collective-permute-start | bytes 786440 | tf_op jit(solution)/shard_map/ppermute | solution.py:491
  59.3 4.3 %collective-permute-start.23 = (bf16[2,256,256]{2,1,0:T(8,128)(2,1)S(1)}, bf16[2,256,256]{2,1,0:T(8,128)(2,1)S(1)}, u32[]{:S(2)}, u32[]{:S(2)}) collective-permute-start(bf16[2,256,256]{2,1,0:T(8,128)(2,1)S(1)} %get-tuple-element.299), channel_id=1, source_target_pairs={{0,2},{2,0},{4,6},{6,4},{1,3},{3,1},{5,7},{7,5},{8,10},{10,8},{12,... | collective-permute-start | bytes 786440 | tf_op jit(solution)/shard_map/ppermute | solution.py:491
  65.2 3.4 %collective-permute-start.21 = (bf16[2,256,256]{2,1,0:T(8,128)(2,1)S(1)}, bf16[2,256,256]{2,1,0:T(8,128)(2,1)S(1)}, u32[]{:S(2)}, u32[]{:S(2)}) collective-permute-start(bf16[2,256,256]{2,1,0:T(8,128)(2,1)S(1)} %get-tuple-element.303), channel_id=1, source_target_pairs={{0,2},{2,0},{4,6},{6,4},{1,3},{3,1},{5,7},{7,5},{8,10},{10,8},{12,... | collective-permute-start | bytes 786440 | tf_op jit(solution)/shard_map/ppermute | solution.py:491
  70.4 3.8 %collective-permute-start.27 = (bf16[2,256,256]{2,1,0:T(8,128)(2,1)S(1)}, bf16[2,256,256]{2,1,0:T(8,128)(2,1)S(1)}, u32[]{:S(2)}, u32[]{:S(2)}) collective-permute-start(bf16[2,256,256]{2,1,0:T(8,128)(2,1)S(1)} %get-tuple-element.311), channel_id=1, source_target_pairs={{0,2},{2,0},{4,6},{6,4},{1,3},{3,1},{5,7},{7,5},{8,10},{10,8},{12,... | collective-permute-start | bytes 786440 | tf_op jit(solution)/shard_map/ppermute | solution.py:491
  76.0 3.9 %collective-permute-start.25 = (bf16[2,256,256]{2,1,0:T(8,128)(2,1)S(1)}, bf16[2,256,256]{2,1,0:T(8,128)(2,1)S(1)}, u32[]{:S(2)}, u32[]{:S(2)}) collective-permute-start(bf16[2,256,256]{2,1,0:T(8,128)(2,1)S(1)} %get-tuple-element.315), channel_id=1, source_target_pairs={{0,2},{2,0},{4,6},{6,4},{1,3},{3,1},{5,7},{7,5},{8,10},{10,8},{12,... | collective-permute-start | bytes 786440 | tf_op jit(solution)/shard_map/ppermute | solution.py:491
  82.3 3.5 %collective-permute-start.31 = (bf16[2,256,256]{2,1,0:T(8,128)(2,1)S(1)}, bf16[2,256,256]{2,1,0:T(8,128)(2,1)S(1)}, u32[]{:S(2)}, u32[]{:S(2)}) collective-permute-start(bf16[2,256,256]{2,1,0:T(8,128)(2,1)S(1)} %get-tuple-element.327), channel_id=1, source_target_pairs={{0,2},{2,0},{4,6},{6,4},{1,3},{3,1},{5,7},{7,5},{8,10},{10,8},{12,... | collective-permute-start | bytes 786440 | tf_op jit(solution)/shard_map/ppermute | solution.py:491
  88.7 3.4 %collective-permute-start.29 = (bf16[2,256,256]{2,1,0:T(8,128)(2,1)S(1)}, bf16[2,256,256]{2,1,0:T(8,128)(2,1)S(1)}, u32[]{:S(2)}, u32[]{:S(2)}) collective-permute-start(bf16[2,256,256]{2,1,0:T(8,128)(2,1)S(1)} %get-tuple-element.331), channel_id=1, source_target_pairs={{0,2},{2,0},{4,6},{6,4},{1,3},{3,1},{5,7},{7,5},{8,10},{10,8},{12,... | collective-permute-start | bytes 786440 | tf_op jit(solution)/shard_map/ppermute | solution.py:491
  106.4 3.9 %collective-permute-start.39 = (bf16[2,256,256]{2,1,0:T(8,128)(2,1)S(1)}, bf16[2,256,256]{2,1,0:T(8,128)(2,1)S(1)}, u32[]{:S(2)}, u32[]{:S(2)}) collective-permute-start(bf16[2,256,256]{2,1,0:T(8,128)(2,1)S(1)} %get-tuple-element.360), channel_id=1, source_target_pairs={{0,2},{2,0},{4,6},{6,4},{1,3},{3,1},{5,7},{7,5},{8,10},{10,8},{12,... | collective-permute-start | bytes 786440 | tf_op jit(solution)/shard_map/ppermute | solution.py:491
  117.2 3.7 %collective-permute-start.43 = (bf16[2,256,256]{2,1,0:T(8,128)(2,1)S(1)}, bf16[2,256,256]{2,1,0:T(8,128)(2,1)S(1)}, u32[]{:S(2)}, u32[]{:S(2)}) collective-permute-start(bf16[2,256,256]{2,1,0:T(8,128)(2,1)S(1)} %get-tuple-element.376), channel_id=1, source_target_pairs={{0,2},{2,0},{4,6},{6,4},{1,3},{3,1},{5,7},{7,5},{8,10},{10,8},{12,... | collective-permute-start | bytes 786440 | tf_op jit(solution)/shard_map/ppermute | solution.py:491
  122.6 4.1 %collective-permute-start.41 = (bf16[2,256,256]{2,1,0:T(8,128)(2,1)S(1)}, bf16[2,256,256]{2,1,0:T(8,128)(2,1)S(1)}, u32[]{:S(2)}, u32[]{:S(2)}) collective-permute-start(bf16[2,256,256]{2,1,0:T(8,128)(2,1)S(1)} %get-tuple-element.380), channel_id=1, source_target_pairs={{0,2},{2,0},{4,6},{6,4},{1,3},{3,1},{5,7},{7,5},{8,10},{10,8},{12,... | collective-permute-start | bytes 786440 | tf_op jit(solution)/shard_map/ppermute | solution.py:491
  128.3 4.1 %collective-permute-start.47 = (bf16[2,256,256]{2,1,0:T(8,128)(2,1)S(1)}, bf16[2,256,256]{2,1,0:T(8,128)(2,1)S(1)}, u32[]{:S(2)}, u32[]{:S(2)}) collective-permute-start(bf16[2,256,256]{2,1,0:T(8,128)(2,1)S(1)} %get-tuple-element.393), channel_id=1, source_target_pairs={{0,2},{2,0},{4,6},{6,4},{1,3},{3,1},{5,7},{7,5},{8,10},{10,8},{12,... | collective-permute-start | bytes 786440 | tf_op jit(solution)/shard_map/ppermute | solution.py:491
  136.7 3.1 %collective-permute-start.45 = (bf16[2,256,256]{2,1,0:T(8,128)(2,1)S(1)}, bf16[2,256,256]{2,1,0:T(8,128)(2,1)S(1)}, u32[]{:S(2)}, u32[]{:S(2)}) collective-permute-start(bf16[2,256,256]{2,1,0:T(8,128)(2,1)S(1)} %get-tuple-element.397), channel_id=1, source_target_pairs={{0,2},{2,0},{4,6},{6,4},{1,3},{3,1},{5,7},{7,5},{8,10},{10,8},{12,... | collective-permute-start | bytes 786440 | tf_op jit(solution)/shard_map/ppermute | solution.py:491
  146.1 4.3 %collective-permute-start.49 = (bf16[2,256,256]{2,1,0:T(8,128)(2,1)S(1)}, bf16[2,256,256]{2,1,0:T(8,128)(2,1)S(1)}, u32[]{:S(2)}, u32[]{:S(2)}) collective-permute-start(bf16[2,256,256]{2,1,0:T(8,128)(2,1)S(1)} %get-tuple-element.414), channel_id=1, source_target_pairs={{0,2},{2,0},{4,6},{6,4},{1,3},{3,1},{5,7},{7,5},{8,10},{10,8},{12,... | collective-permute-start | bytes 786440 | tf_op jit(solution)/shard_map/ppermute | solution.py:491
  151.7 4.5 %collective-permute-start.56 = (bf16[2,256,256]{2,1,0:T(8,128)(2,1)S(1)}, bf16[2,256,256]{2,1,0:T(8,128)(2,1)S(1)}, u32[]{:S(2)}, u32[]{:S(2)}) collective-permute-start(bf16[2,256,256]{2,1,0:T(8,128)(2,1)S(1)} %get-tuple-element.428), channel_id=1, source_target_pairs={{0,2},{2,0},{4,6},{6,4},{1,3},{3,1},{5,7},{7,5},{8,10},{10,8},{12,... | collective-permute-start | bytes 786440 | tf_op jit(solution)/shard_map/ppermute | solution.py:491
  159.7 2.9 %collective-permute-start.54 = (bf16[2,256,256]{2,1,0:T(8,128)(2,1)S(1)}, bf16[2,256,256]{2,1,0:T(8,128)(2,1)S(1)}, u32[]{:S(2)}, u32[]{:S(2)}) collective-permute-start(bf16[2,256,256]{2,1,0:T(8,128)(2,1)S(1)} %get-tuple-element.433), channel_id=1, source_target_pairs={{0,2},{2,0},{4,6},{6,4},{1,3},{3,1},{5,7},{7,5},{8,10},{10,8},{12,... | collective-permute-start | bytes 786440 | tf_op jit(solution)/shard_map/ppermute | solution.py:491
  170.9 3.8 %collective-permute-done.61.outer_2 = bf16[2,256,256]{2,1,0:T(8,128)(2,1)S(1)} collective-permute-done((bf16[2,256,256]{2,1,0:T(8,128)(2,1)S(1)}, bf16[2,256,256]{2,1,0:T(8,128)(2,1)S(1)}, u32[]{:S(2)}, u32[]{:S(2)}) %collective-permute-start.61) | collective-permute-done | bytes 262176 | tf_op jit(solution)/shard_map/ppermute | solution.py:491
  179.6 4.5 %collective-permute-done.59.outer_2 = bf16[2,256,256]{2,1,0:T(8,128)(2,1)S(1)} collective-permute-done((bf16[2,256,256]{2,1,0:T(8,128)(2,1)S(1)}, bf16[2,256,256]{2,1,0:T(8,128)(2,1)S(1)}, u32[]{:S(2)}, u32[]{:S(2)}) %collective-permute-start.59) | collective-permute-done | bytes 262176 | tf_op jit(solution)/shard_map/ppermute | solution.py:491
  193.4 4.0 %shard_map.172 = f32[1536,768]{1,0:T(8,128)} custom-call(f32[512,768]{1,0:T(8,128)S(1)} %shard_map.124.refs_0_, f32[512,768]{1,0:T(8,128)S(1)} %shard_map.139.refs_1_, f32[512,768]{1,0:T(8,128)S(1)} %shard_map.171.refs_2_, bf16[2,2,256,256]{3,2,1,0:T(8,128)(2,1)S(1)} %shard_map.160.done_ref.refs_0_.refs_3_, ...), custom_call_target="tpu_custom_call" | custom-call | flops 1 | bytes 1 | tf_op jit(solution)/shard_map/pallas_call | solution.py:352
  198.4 5.7 %collective-permute-done.64.refs_1_ = bf16[2,128,768]{2,1,0:T(8,128)(2,1)S(1)} collective-permute-done((bf16[2,128,768]{2,1,0:T(8,128)(2,1)S(1)}, bf16[2,128,768]{2,1,0:T(8,128)(2,1)S(1)}, u32[]{:S(2)}, u32[]{:S(2)}) %collective-permute-start.64) | collective-permute-done | bytes 393248 | tf_op jit(solution)/shard_map/ppermute | solution.py:54
  (234 shorter events, 106.3 us)
Async XLA Ops:
  8.3 18.2 %collective-permute-start.2 = (bf16[2,128,768]{2,1,0:T(8,128)(2,1)S(1)}, bf16[2,128,768]{2,1,0:T(8,128)(2,1)S(1)}, u32[]{:S(2)}, u32[]{:S(2)}) collective-permute-start(bf16[2,128,768]{2,1,0:T(8,128)(2,1)S(1)} %pad_maximum_fusion.refs_0_.refs_1_.refs_4_.refs_7_), channel_id=1, source_target_pairs={{0,1},{1,0},{2,3},{3,2},{4,5},{5,4},{6,7},{7,6},{8,9},{9,8},{10,11... | collective-permute-start | bytes 1179656 | tf_op jit(solution)/shard_map/ppermute | solution.py:54
  17.8 14.1 %collective-permute-start.7 = (bf16[2,128,768]{2,1,0:T(8,128)(2,1)S(1)}, bf16[2,128,768]{2,1,0:T(8,128)(2,1)S(1)}, u32[]{:S(2)}, u32[]{:S(2)}) collective-permute-start(bf16[2,128,768]{2,1,0:T(8,128)(2,1)S(1)} %pad_maximum_fusion.refs_0_.refs_1_.refs_4_.refs_7_), channel_id=1, source_target_pairs={{0,16},{8,24},{16,0},{24,8},{1,17},{9,25},{17,1},{25,9},{2,18},{10... | collective-permute-start | bytes 1179656 | tf_op jit(solution)/shard_map/ppermute | solution.py:54
  19.4 12.5 %collective-permute-start.5 = (bf16[2,256,256]{2,1,0:T(8,128)(2,1)S(1)}, bf16[2,256,256]{2,1,0:T(8,128)(2,1)S(1)}, u32[]{:S(2)}, u32[]{:S(2)}) collective-permute-start(bf16[2,256,256]{2,1,0:T(8,128)(2,1)S(1)} %get-tuple-element.257), channel_id=1, source_target_pairs={{0,2},{2,0},{4,6},{6,4},{1,3},{3,1},{5,7},{7,5},{8,10},{10,8},{12,... | collective-permute-start | bytes 786440 | tf_op jit(solution)/shard_map/ppermute | solution.py:491
  26.6 13.1 %collective-permute-start.13 = (bf16[2,256,256]{2,1,0:T(8,128)(2,1)S(1)}, bf16[2,256,256]{2,1,0:T(8,128)(2,1)S(1)}, u32[]{:S(2)}, u32[]{:S(2)}) collective-permute-start(bf16[2,256,256]{2,1,0:T(8,128)(2,1)S(1)} %get-tuple-element.266), channel_id=1, source_target_pairs={{0,2},{2,0},{4,6},{6,4},{1,3},{3,1},{5,7},{7,5},{8,10},{10,8},{12,... | collective-permute-start | bytes 786440 | tf_op jit(solution)/shard_map/ppermute | solution.py:491
  31.9 15.6 %collective-permute-start.11 = (bf16[2,128,768]{2,1,0:T(8,128)(2,1)S(1)}, bf16[2,128,768]{2,1,0:T(8,128)(2,1)S(1)}, u32[]{:S(2)}, u32[]{:S(2)}) collective-permute-start(bf16[2,128,768]{2,1,0:T(8,128)(2,1)S(1)} %collective-permute-done.2.refs_0_.refs_1_), channel_id=1, source_target_pairs={{0,16},{8,24},{16,0},{24,8},{1,17},{9,25},{17,1},{25,9},{2,18},{10... | collective-permute-start | bytes 1179656 | tf_op jit(solution)/shard_map/ppermute | solution.py:54
  35.1 12.4 %collective-permute-start.9 = (bf16[2,256,256]{2,1,0:T(8,128)(2,1)S(1)}, bf16[2,256,256]{2,1,0:T(8,128)(2,1)S(1)}, u32[]{:S(2)}, u32[]{:S(2)}) collective-permute-start(bf16[2,256,256]{2,1,0:T(8,128)(2,1)S(1)} %get-tuple-element.270), channel_id=1, source_target_pairs={{0,2},{2,0},{4,6},{6,4},{1,3},{3,1},{5,7},{7,5},{8,10},{10,8},{12,... | collective-permute-start | bytes 786440 | tf_op jit(solution)/shard_map/ppermute | solution.py:491
  52.5 12.6 %collective-permute-start.17 = (bf16[2,256,256]{2,1,0:T(8,128)(2,1)S(1)}, bf16[2,256,256]{2,1,0:T(8,128)(2,1)S(1)}, u32[]{:S(2)}, u32[]{:S(2)}) collective-permute-start(bf16[2,256,256]{2,1,0:T(8,128)(2,1)S(1)} %get-tuple-element.291), channel_id=1, source_target_pairs={{0,2},{2,0},{4,6},{6,4},{1,3},{3,1},{5,7},{7,5},{8,10},{10,8},{12,... | collective-permute-start | bytes 786440 | tf_op jit(solution)/shard_map/ppermute | solution.py:491
  59.3 11.1 %collective-permute-start.23 = (bf16[2,256,256]{2,1,0:T(8,128)(2,1)S(1)}, bf16[2,256,256]{2,1,0:T(8,128)(2,1)S(1)}, u32[]{:S(2)}, u32[]{:S(2)}) collective-permute-start(bf16[2,256,256]{2,1,0:T(8,128)(2,1)S(1)} %get-tuple-element.299), channel_id=1, source_target_pairs={{0,2},{2,0},{4,6},{6,4},{1,3},{3,1},{5,7},{7,5},{8,10},{10,8},{12,... | collective-permute-start | bytes 786440 | tf_op jit(solution)/shard_map/ppermute | solution.py:491
  70.4 11.8 %collective-permute-start.27 = (bf16[2,256,256]{2,1,0:T(8,128)(2,1)S(1)}, bf16[2,256,256]{2,1,0:T(8,128)(2,1)S(1)}, u32[]{:S(2)}, u32[]{:S(2)}) collective-permute-start(bf16[2,256,256]{2,1,0:T(8,128)(2,1)S(1)} %get-tuple-element.311), channel_id=1, source_target_pairs={{0,2},{2,0},{4,6},{6,4},{1,3},{3,1},{5,7},{7,5},{8,10},{10,8},{12,... | collective-permute-start | bytes 786440 | tf_op jit(solution)/shard_map/ppermute | solution.py:491
  76.0 12.5 %collective-permute-start.25 = (bf16[2,256,256]{2,1,0:T(8,128)(2,1)S(1)}, bf16[2,256,256]{2,1,0:T(8,128)(2,1)S(1)}, u32[]{:S(2)}, u32[]{:S(2)}) collective-permute-start(bf16[2,256,256]{2,1,0:T(8,128)(2,1)S(1)} %get-tuple-element.315), channel_id=1, source_target_pairs={{0,2},{2,0},{4,6},{6,4},{1,3},{3,1},{5,7},{7,5},{8,10},{10,8},{12,... | collective-permute-start | bytes 786440 | tf_op jit(solution)/shard_map/ppermute | solution.py:491
  82.3 13.1 %collective-permute-start.31 = (bf16[2,256,256]{2,1,0:T(8,128)(2,1)S(1)}, bf16[2,256,256]{2,1,0:T(8,128)(2,1)S(1)}, u32[]{:S(2)}, u32[]{:S(2)}) collective-permute-start(bf16[2,256,256]{2,1,0:T(8,128)(2,1)S(1)} %get-tuple-element.327), channel_id=1, source_target_pairs={{0,2},{2,0},{4,6},{6,4},{1,3},{3,1},{5,7},{7,5},{8,10},{10,8},{12,... | collective-permute-start | bytes 786440 | tf_op jit(solution)/shard_map/ppermute | solution.py:491
  99.5 13.6 %collective-permute-start.33 = (bf16[2,256,256]{2,1,0:T(8,128)(2,1)S(1)}, bf16[2,256,256]{2,1,0:T(8,128)(2,1)S(1)}, u32[]{:S(2)}, u32[]{:S(2)}) collective-permute-start(bf16[2,256,256]{2,1,0:T(8,128)(2,1)S(1)} %get-tuple-element.347), channel_id=1, source_target_pairs={{0,2},{2,0},{4,6},{6,4},{1,3},{3,1},{5,7},{7,5},{8,10},{10,8},{12,... | collective-permute-start | bytes 786440 | tf_op jit(solution)/shard_map/ppermute | solution.py:491
  122.6 14.0 %collective-permute-start.41 = (bf16[2,256,256]{2,1,0:T(8,128)(2,1)S(1)}, bf16[2,256,256]{2,1,0:T(8,128)(2,1)S(1)}, u32[]{:S(2)}, u32[]{:S(2)}) collective-permute-start(bf16[2,256,256]{2,1,0:T(8,128)(2,1)S(1)} %get-tuple-element.380), channel_id=1, source_target_pairs={{0,2},{2,0},{4,6},{6,4},{1,3},{3,1},{5,7},{7,5},{8,10},{10,8},{12,... | collective-permute-start | bytes 786440 | tf_op jit(solution)/shard_map/ppermute | solution.py:491
  128.3 12.8 %collective-permute-start.47 = (bf16[2,256,256]{2,1,0:T(8,128)(2,1)S(1)}, bf16[2,256,256]{2,1,0:T(8,128)(2,1)S(1)}, u32[]{:S(2)}, u32[]{:S(2)}) collective-permute-start(bf16[2,256,256]{2,1,0:T(8,128)(2,1)S(1)} %get-tuple-element.393), channel_id=1, source_target_pairs={{0,2},{2,0},{4,6},{6,4},{1,3},{3,1},{5,7},{7,5},{8,10},{10,8},{12,... | collective-permute-start | bytes 786440 | tf_op jit(solution)/shard_map/ppermute | solution.py:491
  135.4 16.2 %collective-permute-start.53 = (bf16[384,512]{1,0:T(8,128)(2,1)S(1)}, bf16[384,512]{1,0:T(8,128)(2,1)S(1)}, u32[]{:S(2)}, u32[]{:S(2)}) collective-permute-start(bf16[384,512]{1,0:T(8,128)(2,1)S(1)} %shard_map.144), channel_id=1, source_target_pairs={{0,1},{1,0},{2,3},{3,2},{4,5},{5,4},{6,7},{7,6},{8,9},{9,8},{10,11... | collective-permute-start | bytes 1179656 | tf_op jit(solution)/shard_map/ppermute | solution.py:54
  146.1 12.3 %collective-permute-start.49 = (bf16[2,256,256]{2,1,0:T(8,128)(2,1)S(1)}, bf16[2,256,256]{2,1,0:T(8,128)(2,1)S(1)}, u32[]{:S(2)}, u32[]{:S(2)}) collective-permute-start(bf16[2,256,256]{2,1,0:T(8,128)(2,1)S(1)} %get-tuple-element.414), channel_id=1, source_target_pairs={{0,2},{2,0},{4,6},{6,4},{1,3},{3,1},{5,7},{7,5},{8,10},{10,8},{12,... | collective-permute-start | bytes 786440 | tf_op jit(solution)/shard_map/ppermute | solution.py:491
  158.3 11.8 %collective-permute-start.58 = (bf16[2,128,768]{2,1,0:T(8,128)(2,1)S(1)}, bf16[2,128,768]{2,1,0:T(8,128)(2,1)S(1)}, u32[]{:S(2)}, u32[]{:S(2)}) collective-permute-start(bf16[2,128,768]{2,1,0:T(8,128)(2,1)S(1)} %get-tuple-element.444), channel_id=1, source_target_pairs={{0,8},{8,0},{16,24},{24,16},{1,9},{9,1},{17,25},{25,17},{2,10},{10... | collective-permute-start | bytes 1179656 | tf_op jit(solution)/shard_map/ppermute | solution.py:54
  159.1 11.8 %collective-permute-start.62 = (bf16[2,128,768]{2,1,0:T(8,128)(2,1)S(1)}, bf16[2,128,768]{2,1,0:T(8,128)(2,1)S(1)}, u32[]{:S(2)}, u32[]{:S(2)}) collective-permute-start(bf16[2,128,768]{2,1,0:T(8,128)(2,1)S(1)} %get-tuple-element.455), channel_id=1, source_target_pairs={{0,8},{8,0},{16,24},{24,16},{1,9},{9,1},{17,25},{25,17},{2,10},{10... | collective-permute-start | bytes 1179656 | tf_op jit(solution)/shard_map/ppermute | solution.py:54
  170.3 15.8 %collective-permute-start.63 = (bf16[2,128,768]{2,1,0:T(8,128)(2,1)S(1)}, bf16[2,128,768]{2,1,0:T(8,128)(2,1)S(1)}, u32[]{:S(2)}, u32[]{:S(2)}) collective-permute-start(bf16[2,128,768]{2,1,0:T(8,128)(2,1)S(1)} %shard_map.158), channel_id=1, source_target_pairs={{0,16},{8,24},{16,0},{24,8},{1,17},{9,25},{17,1},{25,9},{2,18},{10... | collective-permute-start | bytes 1179656 | tf_op jit(solution)/shard_map/ppermute | solution.py:54
  175.4 12.5 %collective-permute-start.65 = (bf16[2,128,768]{2,1,0:T(8,128)(2,1)S(1)}, bf16[2,128,768]{2,1,0:T(8,128)(2,1)S(1)}, u32[]{:S(2)}, u32[]{:S(2)}) collective-permute-start(bf16[2,128,768]{2,1,0:T(8,128)(2,1)S(1)} %get-tuple-element.471), channel_id=1, source_target_pairs={{0,8},{8,0},{16,24},{24,16},{1,9},{9,1},{17,25},{25,17},{2,10},{10... | collective-permute-start | bytes 1179656 | tf_op jit(solution)/shard_map/ppermute | solution.py:54
  184.9 12.6 %collective-permute-start.68 = (bf16[384,512]{1,0:T(8,128)(2,1)S(1)}, bf16[384,512]{1,0:T(8,128)(2,1)S(1)}, u32[]{:S(2)}, u32[]{:S(2)}) collective-permute-start(bf16[384,512]{1,0:T(8,128)(2,1)S(1)} %shard_map.164), channel_id=1, source_target_pairs={{0,1},{1,0},{2,3},{3,2},{4,5},{5,4},{6,7},{7,6},{8,9},{9,8},{10,11... | collective-permute-start | bytes 1179656 | tf_op jit(solution)/shard_map/ppermute | solution.py:54
  186.0 12.3 %collective-permute-start.67 = (bf16[2,128,768]{2,1,0:T(8,128)(2,1)S(1)}, bf16[2,128,768]{2,1,0:T(8,128)(2,1)S(1)}, u32[]{:S(2)}, u32[]{:S(2)}) collective-permute-start(bf16[2,128,768]{2,1,0:T(8,128)(2,1)S(1)} %get-tuple-element.472), channel_id=1, source_target_pairs={{0,8},{8,0},{16,24},{24,16},{1,9},{9,1},{17,25},{25,17},{2,10},{10... | collective-permute-start | bytes 1179656 | tf_op jit(solution)/shard_map/ppermute | solution.py:54
  186.3 17.8 %collective-permute-start.64 = (bf16[2,128,768]{2,1,0:T(8,128)(2,1)S(1)}, bf16[2,128,768]{2,1,0:T(8,128)(2,1)S(1)}, u32[]{:S(2)}, u32[]{:S(2)}) collective-permute-start(bf16[2,128,768]{2,1,0:T(8,128)(2,1)S(1)} %shard_map.159), channel_id=1, source_target_pairs={{0,1},{1,0},{2,3},{3,2},{4,5},{5,4},{6,7},{7,6},{8,9},{9,8},{10,11... | collective-permute-start | bytes 1179656 | tf_op jit(solution)/shard_map/ppermute | solution.py:54
  188.0 16.0 %collective-permute-start.66 = (bf16[2,128,768]{2,1,0:T(8,128)(2,1)S(1)}, bf16[2,128,768]{2,1,0:T(8,128)(2,1)S(1)}, u32[]{:S(2)}, u32[]{:S(2)}) collective-permute-start(bf16[2,128,768]{2,1,0:T(8,128)(2,1)S(1)} %shard_map.162), channel_id=1, source_target_pairs={{0,16},{8,24},{16,0},{24,8},{1,17},{9,25},{17,1},{25,9},{2,18},{10... | collective-permute-start | bytes 1179656 | tf_op jit(solution)/shard_map/ppermute | solution.py:54
  (54 other events, 471.9 us)

commit v2 on v1

--- a/solution.py
+++ b/solution.py
@@ -556,7 +556,7 @@
     if early_start:
         pieces = [(k, True, True) for k in range(4)]
         order = [(0, 0), (1, 0), (0, 1), (0, 2), (0, 3), (1, 3), (1, 1), (1, 2)]
-        order += [(2, 3), (2, 1), (2, 2), (2, 0)]
+        order += [(2, 0), (2, 3), (2, 1), (2, 2)]
         order = [(phase,) + pieces[k] for phase, k in order]
     else:
         pieces = [(0, True, False), (0, False, True)] + [(k, True, True) for k in range(1, 4)]
@@ -618,7 +618,7 @@
                 outputs["own"] = total
             else:
                 stage = (at // own).bit_length() - 1
-                bring(at - (own << stage), total, stages[stage], 6)
+                bring(at - (own << stage), total, stages[stage], 5)
 
     def finish(index, done):
         phase, piece = order[index][0], order[index][1:]
@@ -634,7 +634,7 @@
             ups[phase] = gradient(1, ups[phase], *zip(*kept[phase]))
             downs[phase] = gradient(0, downs[phase], *zip(*kept[phase]))
             want(ups, phase, 4)
-            want(downs, phase, 6)
+            want(downs, phase, 5)
             kept[phase].clear()
         if is_end:
             rest = list(zip(*kept[phase])) or [[], []]
@@ -643,7 +643,7 @@
                 rows = up_rows(row_at[mask], d_rows, ups[phase], *rest, kind)
                 up_blocks[mask][phase] = swap(rows, "depth", mask) if mask else rows
                 if mask and not is_last:
-                    want(up_blocks[mask], phase, 8)
+                    want(up_blocks[mask], phase, 7)
             if is_last:
                 outputs["down"] = all_of_down(factor, downs, *rest)
 

time: 206 us -> 208 us (level)
  waiting for transfers between devices: 31.8 us -> 34.5 us
    ppermute x28, waiting for transfers between devices: 23.6 us -> 26.2 us  [line_swaps(): arrived[0] = lax.ppermute(outer, 'col', [(0, 1), (1, 0), (2, 3), (3, 2)])]
  transfers between devices with their start and end apart: 69 -> 69, of which waited for: 12 -> 16; matrix products, arithmetic and copies ran while one was open for 0% -> 0% of each run, Pallas kernels for 22% -> 22%
where the time goes in v2:
time: 208 us; the launch traced here: 207 us
  starting transfers between devices  117 us (56%)
  Pallas kernels  46.9 us (23%)
  waiting for transfers between devices  34.5 us (17%)
  local copies, waits for them, and re-layouts  5.41 us (3%)
    ppermute x28, starting transfers between devices, line_swaps(): arrived[0] = lax.ppermute(outer, 'col', [(0, 1), (1, 0), (2, 3), (3, 2)])  88.4 us
    pallas_call x92, Pallas kernels, local_kernel(): pl.pallas_call(body, out_shape=out_shapes, in_specs=[IN_SMEM] * len(scala...  34 us
    ppermute x28, waiting for transfers between devices, line_swaps(): arrived[0] = lax.ppermute(outer, 'col', [(0, 1), (1, 0), (2, 3), (3, 2)])  26.2 us
    ppermute x24, starting transfers between devices, line_swaps(): arrived[1] = lax.ppermute(middle, 'col', [(1, 2), (2, 1)])  16.3 us
    ppermute x17, starting transfers between devices, swap(): return lax.ppermute(value, axis, [(i, i ^ mask) for i in range(size)])  12.2 us
    ppermute x17, waiting for transfers between devices, swap(): return lax.ppermute(value, axis, [(i, i ^ mask) for i in range(size)])  8.28 us
    pallas_call x3, Pallas kernels, load(): pl.pallas_call(body, out_shape=[bf16_array(features, size), bf16_array(si...  5.09 us
    unnamed x18, local copies, waits for them, and re-layouts  4.64 us
  transfers between devices with their start and end apart: 69, of which 16 were waited for; matrix products, arithmetic and copies ran while one was open for 0% of the time, Pallas kernels for 22%

profile of v2, /device:TPU:0, one launch (start us, length us, event | category | flops | bytes accessed | tf_op | source)
XLA Modules:
  0.0 206.9 jit_solution(18116176492041991971)
XLA Ops:
  22.5 4.0 %collective-permute-done.1.outer = bf16[2,256,256]{2,1,0:T(8,128)(2,1)S(1)} collective-permute-done((bf16[2,256,256]{2,1,0:T(8,128)(2,1)S(1)}, bf16[2,256,256]{2,1,0:T(8,128)(2,1)S(1)}, u32[]{:S(2)}, u32[]{:S(2)}) %collective-permute-start.1) | collective-permute-done | bytes 262176 | tf_op jit(solution)/shard_map/ppermute | solution.py:491
  27.5 4.4 %collective-permute-done.5.outer = bf16[2,256,256]{2,1,0:T(8,128)(2,1)S(1)} collective-permute-done((bf16[2,256,256]{2,1,0:T(8,128)(2,1)S(1)}, bf16[2,256,256]{2,1,0:T(8,128)(2,1)S(1)}, u32[]{:S(2)}, u32[]{:S(2)}) %collective-permute-start.5) | collective-permute-done | bytes 262176 | tf_op jit(solution)/shard_map/ppermute | solution.py:491
  35.1 4.7 %collective-permute-start.8 = (bf16[2,256,256]{2,1,0:T(8,128)(2,1)S(1)}, bf16[2,256,256]{2,1,0:T(8,128)(2,1)S(1)}, u32[]{:S(2)}, u32[]{:S(2)}) collective-permute-start(bf16[2,256,256]{2,1,0:T(8,128)(2,1)S(1)} %get-tuple-element.271), channel_id=1, source_target_pairs={{0,2},{2,0},{4,6},{6,4},{1,3},{3,1},{5,7},{7,5},{8,10},{10,8},{12,... | collective-permute-start | bytes 786440 | tf_op jit(solution)/shard_map/ppermute | solution.py:491
  41.4 5.4 %collective-permute-start.17 = (bf16[2,256,256]{2,1,0:T(8,128)(2,1)S(1)}, bf16[2,256,256]{2,1,0:T(8,128)(2,1)S(1)}, u32[]{:S(2)}, u32[]{:S(2)}) collective-permute-start(bf16[2,256,256]{2,1,0:T(8,128)(2,1)S(1)} %get-tuple-element.283), channel_id=1, source_target_pairs={{0,2},{2,0},{4,6},{6,4},{1,3},{3,1},{5,7},{7,5},{8,10},{10,8},{12,... | collective-permute-start | bytes 786440 | tf_op jit(solution)/shard_map/ppermute | solution.py:491
  47.7 3.5 %collective-permute-start.15 = (bf16[2,256,256]{2,1,0:T(8,128)(2,1)S(1)}, bf16[2,256,256]{2,1,0:T(8,128)(2,1)S(1)}, u32[]{:S(2)}, u32[]{:S(2)}) collective-permute-start(bf16[2,256,256]{2,1,0:T(8,128)(2,1)S(1)} %get-tuple-element.287), channel_id=1, source_target_pairs={{0,2},{2,0},{4,6},{6,4},{1,3},{3,1},{5,7},{7,5},{8,10},{10,8},{12,... | collective-permute-start | bytes 786440 | tf_op jit(solution)/shard_map/ppermute | solution.py:491
  52.5 4.0 %collective-permute-start.21 = (bf16[2,256,256]{2,1,0:T(8,128)(2,1)S(1)}, bf16[2,256,256]{2,1,0:T(8,128)(2,1)S(1)}, u32[]{:S(2)}, u32[]{:S(2)}) collective-permute-start(bf16[2,256,256]{2,1,0:T(8,128)(2,1)S(1)} %get-tuple-element.295), channel_id=1, source_target_pairs={{0,2},{2,0},{4,6},{6,4},{1,3},{3,1},{5,7},{7,5},{8,10},{10,8},{12,... | collective-permute-start | bytes 786440 | tf_op jit(solution)/shard_map/ppermute | solution.py:491
  59.3 4.3 %collective-permute-start.19 = (bf16[2,256,256]{2,1,0:T(8,128)(2,1)S(1)}, bf16[2,256,256]{2,1,0:T(8,128)(2,1)S(1)}, u32[]{:S(2)}, u32[]{:S(2)}) collective-permute-start(bf16[2,256,256]{2,1,0:T(8,128)(2,1)S(1)} %get-tuple-element.299), channel_id=1, source_target_pairs={{0,2},{2,0},{4,6},{6,4},{1,3},{3,1},{5,7},{7,5},{8,10},{10,8},{12,... | collective-permute-start | bytes 786440 | tf_op jit(solution)/shard_map/ppermute | solution.py:491
  65.2 3.4 %collective-permute-start.25 = (bf16[2,256,256]{2,1,0:T(8,128)(2,1)S(1)}, bf16[2,256,256]{2,1,0:T(8,128)(2,1)S(1)}, u32[]{:S(2)}, u32[]{:S(2)}) collective-permute-start(bf16[2,256,256]{2,1,0:T(8,128)(2,1)S(1)} %get-tuple-element.307), channel_id=1, source_target_pairs={{0,2},{2,0},{4,6},{6,4},{1,3},{3,1},{5,7},{7,5},{8,10},{10,8},{12,... | collective-permute-start | bytes 786440 | tf_op jit(solution)/shard_map/ppermute | solution.py:491
  70.4 3.8 %collective-permute-start.23 = (bf16[2,256,256]{2,1,0:T(8,128)(2,1)S(1)}, bf16[2,256,256]{2,1,0:T(8,128)(2,1)S(1)}, u32[]{:S(2)}, u32[]{:S(2)}) collective-permute-start(bf16[2,256,256]{2,1,0:T(8,128)(2,1)S(1)} %get-tuple-element.311), channel_id=1, source_target_pairs={{0,2},{2,0},{4,6},{6,4},{1,3},{3,1},{5,7},{7,5},{8,10},{10,8},{12,... | collective-permute-start | bytes 786440 | tf_op jit(solution)/shard_map/ppermute | solution.py:491
  76.0 3.9 %collective-permute-start.29 = (bf16[2,256,256]{2,1,0:T(8,128)(2,1)S(1)}, bf16[2,256,256]{2,1,0:T(8,128)(2,1)S(1)}, u32[]{:S(2)}, u32[]{:S(2)}) collective-permute-start(bf16[2,256,256]{2,1,0:T(8,128)(2,1)S(1)} %get-tuple-element.320), channel_id=1, source_target_pairs={{0,2},{2,0},{4,6},{6,4},{1,3},{3,1},{5,7},{7,5},{8,10},{10,8},{12,... | collective-permute-start | bytes 786440 | tf_op jit(solution)/shard_map/ppermute | solution.py:491
  82.3 3.4 %collective-permute-start.27 = (bf16[2,256,256]{2,1,0:T(8,128)(2,1)S(1)}, bf16[2,256,256]{2,1,0:T(8,128)(2,1)S(1)}, u32[]{:S(2)}, u32[]{:S(2)}) collective-permute-start(bf16[2,256,256]{2,1,0:T(8,128)(2,1)S(1)} %get-tuple-element.324), channel_id=1, source_target_pairs={{0,2},{2,0},{4,6},{6,4},{1,3},{3,1},{5,7},{7,5},{8,10},{10,8},{12,... | collective-permute-start | bytes 786440 | tf_op jit(solution)/shard_map/ppermute | solution.py:491
  90.0 3.4 %collective-permute-start.33 = (bf16[2,256,256]{2,1,0:T(8,128)(2,1)S(1)}, bf16[2,256,256]{2,1,0:T(8,128)(2,1)S(1)}, u32[]{:S(2)}, u32[]{:S(2)}) collective-permute-start(bf16[2,256,256]{2,1,0:T(8,128)(2,1)S(1)} %get-tuple-element.338), channel_id=1, source_target_pairs={{0,2},{2,0},{4,6},{6,4},{1,3},{3,1},{5,7},{7,5},{8,10},{10,8},{12,... | collective-permute-start | bytes 786440 | tf_op jit(solution)/shard_map/ppermute | solution.py:491
  100.0 4.6 %collective-permute-start.37 = (bf16[2,256,256]{2,1,0:T(8,128)(2,1)S(1)}, bf16[2,256,256]{2,1,0:T(8,128)(2,1)S(1)}, u32[]{:S(2)}, u32[]{:S(2)}) collective-permute-start(bf16[2,256,256]{2,1,0:T(8,128)(2,1)S(1)} %get-tuple-element.352), channel_id=1, source_target_pairs={{0,2},{2,0},{4,6},{6,4},{1,3},{3,1},{5,7},{7,5},{8,10},{10,8},{12,... | collective-permute-start | bytes 786440 | tf_op jit(solution)/shard_map/ppermute | solution.py:491
  115.2 2.9 %collective-permute-start.41 = (bf16[2,256,256]{2,1,0:T(8,128)(2,1)S(1)}, bf16[2,256,256]{2,1,0:T(8,128)(2,1)S(1)}, u32[]{:S(2)}, u32[]{:S(2)}) collective-permute-start(bf16[2,256,256]{2,1,0:T(8,128)(2,1)S(1)} %get-tuple-element.372), channel_id=1, source_target_pairs={{0,2},{2,0},{4,6},{6,4},{1,3},{3,1},{5,7},{7,5},{8,10},{10,8},{12,... | collective-permute-start | bytes 786440 | tf_op jit(solution)/shard_map/ppermute | solution.py:491
  124.4 4.3 %collective-permute-start.45 = (bf16[2,256,256]{2,1,0:T(8,128)(2,1)S(1)}, bf16[2,256,256]{2,1,0:T(8,128)(2,1)S(1)}, u32[]{:S(2)}, u32[]{:S(2)}) collective-permute-start(bf16[2,256,256]{2,1,0:T(8,128)(2,1)S(1)} %get-tuple-element.384), channel_id=1, source_target_pairs={{0,2},{2,0},{4,6},{6,4},{1,3},{3,1},{5,7},{7,5},{8,10},{10,8},{12,... | collective-permute-start | bytes 786440 | tf_op jit(solution)/shard_map/ppermute | solution.py:491
  130.4 4.1 %collective-permute-start.43 = (bf16[2,256,256]{2,1,0:T(8,128)(2,1)S(1)}, bf16[2,256,256]{2,1,0:T(8,128)(2,1)S(1)}, u32[]{:S(2)}, u32[]{:S(2)}) collective-permute-start(bf16[2,256,256]{2,1,0:T(8,128)(2,1)S(1)} %get-tuple-element.389), channel_id=1, source_target_pairs={{0,2},{2,0},{4,6},{6,4},{1,3},{3,1},{5,7},{7,5},{8,10},{10,8},{12,... | collective-permute-start | bytes 786440 | tf_op jit(solution)/shard_map/ppermute | solution.py:491
  138.7 2.9 %collective-permute-start.49 = (bf16[2,256,256]{2,1,0:T(8,128)(2,1)S(1)}, bf16[2,256,256]{2,1,0:T(8,128)(2,1)S(1)}, u32[]{:S(2)}, u32[]{:S(2)}) collective-permute-start(bf16[2,256,256]{2,1,0:T(8,128)(2,1)S(1)} %get-tuple-element.407), channel_id=1, source_target_pairs={{0,2},{2,0},{4,6},{6,4},{1,3},{3,1},{5,7},{7,5},{8,10},{10,8},{12,... | collective-permute-start | bytes 786440 | tf_op jit(solution)/shard_map/ppermute | solution.py:491
  147.8 4.4 %collective-permute-start.52 = (bf16[2,256,256]{2,1,0:T(8,128)(2,1)S(1)}, bf16[2,256,256]{2,1,0:T(8,128)(2,1)S(1)}, u32[]{:S(2)}, u32[]{:S(2)}) collective-permute-start(bf16[2,256,256]{2,1,0:T(8,128)(2,1)S(1)} %get-tuple-element.421), channel_id=1, source_target_pairs={{0,2},{2,0},{4,6},{6,4},{1,3},{3,1},{5,7},{7,5},{8,10},{10,8},{12,... | collective-permute-start | bytes 786440 | tf_op jit(solution)/shard_map/ppermute | solution.py:491
  154.2 4.3 %collective-permute-start.57 = (bf16[2,256,256]{2,1,0:T(8,128)(2,1)S(1)}, bf16[2,256,256]{2,1,0:T(8,128)(2,1)S(1)}, u32[]{:S(2)}, u32[]{:S(2)}) collective-permute-start(bf16[2,256,256]{2,1,0:T(8,128)(2,1)S(1)} %get-tuple-element.435), channel_id=1, source_target_pairs={{0,2},{2,0},{4,6},{6,4},{1,3},{3,1},{5,7},{7,5},{8,10},{10,8},{12,... | collective-permute-start | bytes 786440 | tf_op jit(solution)/shard_map/ppermute | solution.py:491
  160.8 3.0 %collective-permute-start.54 = (bf16[2,256,256]{2,1,0:T(8,128)(2,1)S(1)}, bf16[2,256,256]{2,1,0:T(8,128)(2,1)S(1)}, u32[]{:S(2)}, u32[]{:S(2)}) collective-permute-start(bf16[2,256,256]{2,1,0:T(8,128)(2,1)S(1)} %get-tuple-element.439), channel_id=1, source_target_pairs={{0,2},{2,0},{4,6},{6,4},{1,3},{3,1},{5,7},{7,5},{8,10},{10,8},{12,... | collective-permute-start | bytes 786440 | tf_op jit(solution)/shard_map/ppermute | solution.py:491
  167.2 3.5 %collective-permute-done.54.outer = bf16[2,256,256]{2,1,0:T(8,128)(2,1)S(1)} collective-permute-done((bf16[2,256,256]{2,1,0:T(8,128)(2,1)S(1)}, bf16[2,256,256]{2,1,0:T(8,128)(2,1)S(1)}, u32[]{:S(2)}, u32[]{:S(2)}) %collective-permute-start.54) | collective-permute-done | bytes 262176 | tf_op jit(solution)/shard_map/ppermute | solution.py:491
  180.7 3.8 %collective-permute-done.65.outer_2 = bf16[2,256,256]{2,1,0:T(8,128)(2,1)S(1)} collective-permute-done((bf16[2,256,256]{2,1,0:T(8,128)(2,1)S(1)}, bf16[2,256,256]{2,1,0:T(8,128)(2,1)S(1)}, u32[]{:S(2)}, u32[]{:S(2)}) %collective-permute-start.65) | collective-permute-done | bytes 262176 | tf_op jit(solution)/shard_map/ppermute | solution.py:491
  193.1 4.0 %shard_map.172 = f32[1536,768]{1,0:T(8,128)} custom-call(f32[512,768]{1,0:T(8,128)S(1)} %shard_map.119.refs_0_, f32[512,768]{1,0:T(8,128)S(1)} %shard_map.137.refs_1_, f32[512,768]{1,0:T(8,128)S(1)} %shard_map.161.refs_2_, bf16[2,2,256,256]{3,2,1,0:T(8,128)(2,1)S(1)} %shard_map.156.done_ref.refs_0_.refs_3_, ...), custom_call_target="tpu_custom_call" | custom-call | flops 1 | bytes 1 | tf_op jit(solution)/shard_map/pallas_call | solution.py:352
  198.8 7.1 %collective-permute-done.64.refs_2_ = bf16[2,128,768]{2,1,0:T(8,128)(2,1)S(1)} collective-permute-done((bf16[2,128,768]{2,1,0:T(8,128)(2,1)S(1)}, bf16[2,128,768]{2,1,0:T(8,128)(2,1)S(1)}, u32[]{:S(2)}, u32[]{:S(2)}) %collective-permute-start.64) | collective-permute-done | bytes 393248 | tf_op jit(solution)/shard_map/ppermute | solution.py:54
  (234 shorter events, 107.6 us)
Async XLA Ops:
  8.3 18.2 %collective-permute-start.2 = (bf16[2,128,768]{2,1,0:T(8,128)(2,1)S(1)}, bf16[2,128,768]{2,1,0:T(8,128)(2,1)S(1)}, u32[]{:S(2)}, u32[]{:S(2)}) collective-permute-start(bf16[2,128,768]{2,1,0:T(8,128)(2,1)S(1)} %pad_maximum_fusion.refs_0_.refs_1_), channel_id=1, source_target_pairs={{0,1},{1,0},{2,3},{3,2},{4,5},{5,4},{6,7},{7,6},{8,9},{9,8},{10,11... | collective-permute-start | bytes 1179656 | tf_op jit(solution)/shard_map/ppermute | solution.py:54
  17.8 14.1 %collective-permute-start.7 = (bf16[2,128,768]{2,1,0:T(8,128)(2,1)S(1)}, bf16[2,128,768]{2,1,0:T(8,128)(2,1)S(1)}, u32[]{:S(2)}, u32[]{:S(2)}) collective-permute-start(bf16[2,128,768]{2,1,0:T(8,128)(2,1)S(1)} %pad_maximum_fusion.refs_0_.refs_1_), channel_id=1, source_target_pairs={{0,16},{8,24},{16,0},{24,8},{1,17},{9,25},{17,1},{25,9},{2,18},{10... | collective-permute-start | bytes 1179656 | tf_op jit(solution)/shard_map/ppermute | solution.py:54
  19.4 12.5 %collective-permute-start.5 = (bf16[2,256,256]{2,1,0:T(8,128)(2,1)S(1)}, bf16[2,256,256]{2,1,0:T(8,128)(2,1)S(1)}, u32[]{:S(2)}, u32[]{:S(2)}) collective-permute-start(bf16[2,256,256]{2,1,0:T(8,128)(2,1)S(1)} %get-tuple-element.259), channel_id=1, source_target_pairs={{0,2},{2,0},{4,6},{6,4},{1,3},{3,1},{5,7},{7,5},{8,10},{10,8},{12,... | collective-permute-start | bytes 786440 | tf_op jit(solution)/shard_map/ppermute | solution.py:491
  26.6 13.1 %collective-permute-start.12 = (bf16[2,256,256]{2,1,0:T(8,128)(2,1)S(1)}, bf16[2,256,256]{2,1,0:T(8,128)(2,1)S(1)}, u32[]{:S(2)}, u32[]{:S(2)}) collective-permute-start(bf16[2,256,256]{2,1,0:T(8,128)(2,1)S(1)} %get-tuple-element.267), channel_id=1, source_target_pairs={{0,2},{2,0},{4,6},{6,4},{1,3},{3,1},{5,7},{7,5},{8,10},{10,8},{12,... | collective-permute-start | bytes 786440 | tf_op jit(solution)/shard_map/ppermute | solution.py:491
  31.9 15.6 %collective-permute-start.10 = (bf16[2,128,768]{2,1,0:T(8,128)(2,1)S(1)}, bf16[2,128,768]{2,1,0:T(8,128)(2,1)S(1)}, u32[]{:S(2)}, u32[]{:S(2)}) collective-permute-start(bf16[2,128,768]{2,1,0:T(8,128)(2,1)S(1)} %collective-permute-done.2.refs_0_.refs_1_.refs_2_.refs_5_), channel_id=1, source_target_pairs={{0,16},{8,24},{16,0},{24,8},{1,17},{9,25},{17,1},{25,9},{2,18},{10... | collective-permute-start | bytes 1179656 | tf_op jit(solution)/shard_map/ppermute | solution.py:54
  35.1 12.4 %collective-permute-start.8 = (bf16[2,256,256]{2,1,0:T(8,128)(2,1)S(1)}, bf16[2,256,256]{2,1,0:T(8,128)(2,1)S(1)}, u32[]{:S(2)}, u32[]{:S(2)}) collective-permute-start(bf16[2,256,256]{2,1,0:T(8,128)(2,1)S(1)} %get-tuple-element.271), channel_id=1, source_target_pairs={{0,2},{2,0},{4,6},{6,4},{1,3},{3,1},{5,7},{7,5},{8,10},{10,8},{12,... | collective-permute-start | bytes 786440 | tf_op jit(solution)/shard_map/ppermute | solution.py:491
  52.5 12.5 %collective-permute-start.21 = (bf16[2,256,256]{2,1,0:T(8,128)(2,1)S(1)}, bf16[2,256,256]{2,1,0:T(8,128)(2,1)S(1)}, u32[]{:S(2)}, u32[]{:S(2)}) collective-permute-start(bf16[2,256,256]{2,1,0:T(8,128)(2,1)S(1)} %get-tuple-element.295), channel_id=1, source_target_pairs={{0,2},{2,0},{4,6},{6,4},{1,3},{3,1},{5,7},{7,5},{8,10},{10,8},{12,... | collective-permute-start | bytes 786440 | tf_op jit(solution)/shard_map/ppermute | solution.py:491
  70.4 11.8 %collective-permute-start.23 = (bf16[2,256,256]{2,1,0:T(8,128)(2,1)S(1)}, bf16[2,256,256]{2,1,0:T(8,128)(2,1)S(1)}, u32[]{:S(2)}, u32[]{:S(2)}) collective-permute-start(bf16[2,256,256]{2,1,0:T(8,128)(2,1)S(1)} %get-tuple-element.311), channel_id=1, source_target_pairs={{0,2},{2,0},{4,6},{6,4},{1,3},{3,1},{5,7},{7,5},{8,10},{10,8},{12,... | collective-permute-start | bytes 786440 | tf_op jit(solution)/shard_map/ppermute | solution.py:491
  76.0 13.8 %collective-permute-start.29 = (bf16[2,256,256]{2,1,0:T(8,128)(2,1)S(1)}, bf16[2,256,256]{2,1,0:T(8,128)(2,1)S(1)}, u32[]{:S(2)}, u32[]{:S(2)}) collective-permute-start(bf16[2,256,256]{2,1,0:T(8,128)(2,1)S(1)} %get-tuple-element.320), channel_id=1, source_target_pairs={{0,2},{2,0},{4,6},{6,4},{1,3},{3,1},{5,7},{7,5},{8,10},{10,8},{12,... | collective-permute-start | bytes 786440 | tf_op jit(solution)/shard_map/ppermute | solution.py:491
  82.3 13.1 %collective-permute-start.27 = (bf16[2,256,256]{2,1,0:T(8,128)(2,1)S(1)}, bf16[2,256,256]{2,1,0:T(8,128)(2,1)S(1)}, u32[]{:S(2)}, u32[]{:S(2)}) collective-permute-start(bf16[2,256,256]{2,1,0:T(8,128)(2,1)S(1)} %get-tuple-element.324), channel_id=1, source_target_pairs={{0,2},{2,0},{4,6},{6,4},{1,3},{3,1},{5,7},{7,5},{8,10},{10,8},{12,... | collective-permute-start | bytes 786440 | tf_op jit(solution)/shard_map/ppermute | solution.py:491
  95.5 13.2 %collective-permute-start.31 = (bf16[2,256,256]{2,1,0:T(8,128)(2,1)S(1)}, bf16[2,256,256]{2,1,0:T(8,128)(2,1)S(1)}, u32[]{:S(2)}, u32[]{:S(2)}) collective-permute-start(bf16[2,256,256]{2,1,0:T(8,128)(2,1)S(1)} %get-tuple-element.342), channel_id=1, source_target_pairs={{0,2},{2,0},{4,6},{6,4},{1,3},{3,1},{5,7},{7,5},{8,10},{10,8},{12,... | collective-permute-start | bytes 786440 | tf_op jit(solution)/shard_map/ppermute | solution.py:491
  97.4 11.4 %collective-permute-start.32 = (bf16[2,256,256]{2,1,0:T(8,128)(2,1)S(1)}, bf16[2,256,256]{2,1,0:T(8,128)(2,1)S(1)}, u32[]{:S(2)}, u32[]{:S(2)}) collective-permute-start(bf16[2,256,256]{2,1,0:T(8,128)(2,1)S(1)} %get-tuple-element.343), channel_id=1, source_target_pairs={{2,4},{4,2},{3,5},{5,3},{10,12},{12,10},{11,13},{13,11},{18,20},{2... | collective-permute-start | bytes 786440 | tf_op jit(solution)/shard_map/ppermute | solution.py:493
  100.0 15.1 %collective-permute-start.37 = (bf16[2,256,256]{2,1,0:T(8,128)(2,1)S(1)}, bf16[2,256,256]{2,1,0:T(8,128)(2,1)S(1)}, u32[]{:S(2)}, u32[]{:S(2)}) collective-permute-start(bf16[2,256,256]{2,1,0:T(8,128)(2,1)S(1)} %get-tuple-element.352), channel_id=1, source_target_pairs={{0,2},{2,0},{4,6},{6,4},{1,3},{3,1},{5,7},{7,5},{8,10},{10,8},{12,... | collective-permute-start | bytes 786440 | tf_op jit(solution)/shard_map/ppermute | solution.py:491
  124.4 14.3 %collective-permute-start.45 = (bf16[2,256,256]{2,1,0:T(8,128)(2,1)S(1)}, bf16[2,256,256]{2,1,0:T(8,128)(2,1)S(1)}, u32[]{:S(2)}, u32[]{:S(2)}) collective-permute-start(bf16[2,256,256]{2,1,0:T(8,128)(2,1)S(1)} %get-tuple-element.384), channel_id=1, source_target_pairs={{0,2},{2,0},{4,6},{6,4},{1,3},{3,1},{5,7},{7,5},{8,10},{10,8},{12,... | collective-permute-start | bytes 786440 | tf_op jit(solution)/shard_map/ppermute | solution.py:491
  130.4 14.4 %collective-permute-start.43 = (bf16[2,256,256]{2,1,0:T(8,128)(2,1)S(1)}, bf16[2,256,256]{2,1,0:T(8,128)(2,1)S(1)}, u32[]{:S(2)}, u32[]{:S(2)}) collective-permute-start(bf16[2,256,256]{2,1,0:T(8,128)(2,1)S(1)} %get-tuple-element.389), channel_id=1, source_target_pairs={{0,2},{2,0},{4,6},{6,4},{1,3},{3,1},{5,7},{7,5},{8,10},{10,8},{12,... | collective-permute-start | bytes 786440 | tf_op jit(solution)/shard_map/ppermute | solution.py:491
  135.2 12.4 %collective-permute-start.51 = (bf16[384,512]{1,0:T(8,128)(2,1)S(1)}, bf16[384,512]{1,0:T(8,128)(2,1)S(1)}, u32[]{:S(2)}, u32[]{:S(2)}) collective-permute-start(bf16[384,512]{1,0:T(8,128)(2,1)S(1)} %shard_map.143), channel_id=1, source_target_pairs={{0,1},{1,0},{2,3},{3,2},{4,5},{5,4},{6,7},{7,6},{8,9},{9,8},{10,11... | collective-permute-start | bytes 1179656 | tf_op jit(solution)/shard_map/ppermute | solution.py:54
  147.8 12.9 %collective-permute-start.52 = (bf16[2,256,256]{2,1,0:T(8,128)(2,1)S(1)}, bf16[2,256,256]{2,1,0:T(8,128)(2,1)S(1)}, u32[]{:S(2)}, u32[]{:S(2)}) collective-permute-start(bf16[2,256,256]{2,1,0:T(8,128)(2,1)S(1)} %get-tuple-element.421), channel_id=1, source_target_pairs={{0,2},{2,0},{4,6},{6,4},{1,3},{3,1},{5,7},{7,5},{8,10},{10,8},{12,... | collective-permute-start | bytes 786440 | tf_op jit(solution)/shard_map/ppermute | solution.py:491
  160.1 12.4 %collective-permute-start.56 = (bf16[2,128,768]{2,1,0:T(8,128)(2,1)S(1)}, bf16[2,128,768]{2,1,0:T(8,128)(2,1)S(1)}, u32[]{:S(2)}, u32[]{:S(2)}) collective-permute-start(bf16[2,128,768]{2,1,0:T(8,128)(2,1)S(1)} %get-tuple-element.441), channel_id=1, source_target_pairs={{0,8},{8,0},{16,24},{24,16},{1,9},{9,1},{17,25},{25,17},{2,10},{10... | collective-permute-start | bytes 1179656 | tf_op jit(solution)/shard_map/ppermute | solution.py:54
  165.2 11.7 %collective-permute-start.61 = (bf16[2,128,768]{2,1,0:T(8,128)(2,1)S(1)}, bf16[2,128,768]{2,1,0:T(8,128)(2,1)S(1)}, u32[]{:S(2)}, u32[]{:S(2)}) collective-permute-start(bf16[2,128,768]{2,1,0:T(8,128)(2,1)S(1)} %get-tuple-element.456), channel_id=1, source_target_pairs={{0,8},{8,0},{16,24},{24,16},{1,9},{9,1},{17,25},{25,17},{2,10},{10... | collective-permute-start | bytes 1179656 | tf_op jit(solution)/shard_map/ppermute | solution.py:54
  165.5 12.1 %collective-permute-start.60 = (bf16[384,512]{1,0:T(8,128)(2,1)S(1)}, bf16[384,512]{1,0:T(8,128)(2,1)S(1)}, u32[]{:S(2)}, u32[]{:S(2)}) collective-permute-start(bf16[384,512]{1,0:T(8,128)(2,1)S(1)} %shard_map.151), channel_id=1, source_target_pairs={{0,1},{1,0},{2,3},{3,2},{4,5},{5,4},{6,7},{7,6},{8,9},{9,8},{10,11... | collective-permute-start | bytes 1179656 | tf_op jit(solution)/shard_map/ppermute | solution.py:54
  172.5 12.0 %collective-permute-start.65 = (bf16[2,256,256]{2,1,0:T(8,128)(2,1)S(1)}, bf16[2,256,256]{2,1,0:T(8,128)(2,1)S(1)}, u32[]{:S(2)}, u32[]{:S(2)}) collective-permute-start(bf16[2,256,256]{2,1,0:T(8,128)(2,1)S(1)} %collective-permute-done.55.middle), channel_id=1, source_target_pairs={{0,2},{2,0},{4,6},{6,4},{1,3},{3,1},{5,7},{7,5},{8,10},{10,8},{12,... | collective-permute-start | bytes 786440 | tf_op jit(solution)/shard_map/ppermute | solution.py:491
  185.9 12.0 %collective-permute-start.68 = (bf16[384,512]{1,0:T(8,128)(2,1)S(1)}, bf16[384,512]{1,0:T(8,128)(2,1)S(1)}, u32[]{:S(2)}, u32[]{:S(2)}) collective-permute-start(bf16[384,512]{1,0:T(8,128)(2,1)S(1)} %shard_map.166), channel_id=1, source_target_pairs={{0,1},{1,0},{2,3},{3,2},{4,5},{5,4},{6,7},{7,6},{8,9},{9,8},{10,11... | collective-permute-start | bytes 1179656 | tf_op jit(solution)/shard_map/ppermute | solution.py:54
  187.6 18.2 %collective-permute-start.64 = (bf16[2,128,768]{2,1,0:T(8,128)(2,1)S(1)}, bf16[2,128,768]{2,1,0:T(8,128)(2,1)S(1)}, u32[]{:S(2)}, u32[]{:S(2)}) collective-permute-start(bf16[2,128,768]{2,1,0:T(8,128)(2,1)S(1)} %shard_map.159), channel_id=1, source_target_pairs={{0,1},{1,0},{2,3},{3,2},{4,5},{5,4},{6,7},{7,6},{8,9},{9,8},{10,11... | collective-permute-start | bytes 1179656 | tf_op jit(solution)/shard_map/ppermute | solution.py:54
  188.9 16.9 %collective-permute-start.67 = (bf16[2,128,768]{2,1,0:T(8,128)(2,1)S(1)}, bf16[2,128,768]{2,1,0:T(8,128)(2,1)S(1)}, u32[]{:S(2)}, u32[]{:S(2)}) collective-permute-start(bf16[2,128,768]{2,1,0:T(8,128)(2,1)S(1)} %shard_map.164), channel_id=1, source_target_pairs={{0,16},{8,24},{16,0},{24,8},{1,17},{9,25},{17,1},{25,9},{2,18},{10... | collective-permute-start | bytes 1179656 | tf_op jit(solution)/shard_map/ppermute | solution.py:54
  (54 other events, 475.9 us)

commit v3 on v1

--- a/solution.py
+++ b/solution.py
@@ -618,7 +618,7 @@
                 outputs["own"] = total
             else:
                 stage = (at // own).bit_length() - 1
-                bring(at - (own << stage), total, stages[stage], 6)
+                bring(at - (own << stage), total, stages[stage], 6 if k == 1 else 6)
 
     def finish(index, done):
         phase, piece = order[index][0], order[index][1:]
@@ -633,8 +633,8 @@
         if not is_rest and (count >= 2 * unit or is_end):
             ups[phase] = gradient(1, ups[phase], *zip(*kept[phase]))
             downs[phase] = gradient(0, downs[phase], *zip(*kept[phase]))
-            want(ups, phase, 4)
-            want(downs, phase, 6)
+            want(ups, phase, 5)
+            want(downs, phase, 7)
             kept[phase].clear()
         if is_end:
             rest = list(zip(*kept[phase])) or [[], []]
@@ -643,7 +643,7 @@
                 rows = up_rows(row_at[mask], d_rows, ups[phase], *rest, kind)
                 up_blocks[mask][phase] = swap(rows, "depth", mask) if mask else rows
                 if mask and not is_last:
-                    want(up_blocks[mask], phase, 8)
+                    want(up_blocks[mask], phase, 9)
             if is_last:
                 outputs["down"] = all_of_down(factor, downs, *rest)
 
@@ -655,7 +655,7 @@
             send(piece, outputs[piece])
         else:
             for part in range(len(sizes)):
-                want(outputs[piece], part, 5)
+                want(outputs[piece], part, 6)
 
     streams = [
         line(place, range(stream, len(order), STREAMS), take, finish) for stream in range(STREAMS)

time: 206 us -> 208 us (level)
  waiting for transfers between devices: 31.8 us -> 41.9 us
  starting transfers between devices: 118 us -> 109 us
    ppermute x28, waiting for transfers between devices: 23.6 us -> 34.2 us  [line_swaps(): arrived[0] = lax.ppermute(outer, 'col', [(0, 1), (1, 0), (2, 3), (3, 2)])]
    ppermute x28, starting transfers between devices: 89.8 us -> 81.4 us  [line_swaps(): arrived[0] = lax.ppermute(outer, 'col', [(0, 1), (1, 0), (2, 3), (3, 2)])]
  transfers between devices with their start and end apart: 69 -> 69, of which waited for: 12 -> 17; matrix products, arithmetic and copies ran while one was open for 0% -> 0% of each run, Pallas kernels for 22% -> 22%
where the time goes in v3:
time: 208 us; the launch traced here: 207 us
  starting transfers between devices  109 us (52%)
  Pallas kernels  46.9 us (23%)
  waiting for transfers between devices  41.9 us (20%)
  local copies, waits for them, and re-layouts  5.41 us (3%)
    ppermute x28, starting transfers between devices, line_swaps(): arrived[0] = lax.ppermute(outer, 'col', [(0, 1), (1, 0), (2, 3), (3, 2)])  81.4 us
    ppermute x28, waiting for transfers between devices, line_swaps(): arrived[0] = lax.ppermute(outer, 'col', [(0, 1), (1, 0), (2, 3), (3, 2)])  34.2 us
    pallas_call x92, Pallas kernels, local_kernel(): pl.pallas_call(body, out_shape=out_shapes, in_specs=[IN_SMEM] * len(scala...  34 us
    ppermute x24, starting transfers between devices, line_swaps(): arrived[1] = lax.ppermute(middle, 'col', [(1, 2), (2, 1)])  16.2 us
    ppermute x17, starting transfers between devices, swap(): return lax.ppermute(value, axis, [(i, i ^ mask) for i in range(size)])  11.8 us
    ppermute x17, waiting for transfers between devices, swap(): return lax.ppermute(value, axis, [(i, i ^ mask) for i in range(size)])  7.63 us
    pallas_call x3, Pallas kernels, load(): pl.pallas_call(body, out_shape=[bf16_array(features, size), bf16_array(si...  5.09 us
    unnamed x18, local copies, waits for them, and re-layouts  4.64 us
  transfers between devices with their start and end apart: 69, of which 17 were waited for; matrix products, arithmetic and copies ran while one was open for 0% of the time, Pallas kernels for 22%

profile of v3, /device:TPU:0, one launch (start us, length us, event | category | flops | bytes accessed | tf_op | source)
XLA Modules:
  0.0 206.8 jit_solution(12973994019565858039)
XLA Ops:
  8.3 2.9 %collective-permute-start.2 = (bf16[2,128,768]{2,1,0:T(8,128)(2,1)S(1)}, bf16[2,128,768]{2,1,0:T(8,128)(2,1)S(1)}, u32[]{:S(2)}, u32[]{:S(2)}) collective-permute-start(bf16[2,128,768]{2,1,0:T(8,128)(2,1)S(1)} %pad_maximum_fusion.refs_0_.refs_1_.refs_4_.refs_7_), channel_id=1, source_target_pairs={{0,1},{1,0},{2,3},{3,2},{4,5},{5,4},{6,7},{7,6},{8,9},{9,8},{10,11... | collective-permute-start | bytes 1179656 | tf_op jit(solution)/shard_map/ppermute | solution.py:54
  22.5 4.0 %collective-permute-done.1.outer = bf16[2,256,256]{2,1,0:T(8,128)(2,1)S(1)} collective-permute-done((bf16[2,256,256]{2,1,0:T(8,128)(2,1)S(1)}, bf16[2,256,256]{2,1,0:T(8,128)(2,1)S(1)}, u32[]{:S(2)}, u32[]{:S(2)}) %collective-permute-start.1) | collective-permute-done | bytes 262176 | tf_op jit(solution)/shard_map/ppermute | solution.py:491
  27.5 4.4 %collective-permute-done.5.outer = bf16[2,256,256]{2,1,0:T(8,128)(2,1)S(1)} collective-permute-done((bf16[2,256,256]{2,1,0:T(8,128)(2,1)S(1)}, bf16[2,256,256]{2,1,0:T(8,128)(2,1)S(1)}, u32[]{:S(2)}, u32[]{:S(2)}) %collective-permute-start.5) | collective-permute-done | bytes 262176 | tf_op jit(solution)/shard_map/ppermute | solution.py:491
  36.5 5.2 %collective-permute-start.9 = (bf16[2,256,256]{2,1,0:T(8,128)(2,1)S(1)}, bf16[2,256,256]{2,1,0:T(8,128)(2,1)S(1)}, u32[]{:S(2)}, u32[]{:S(2)}) collective-permute-start(bf16[2,256,256]{2,1,0:T(8,128)(2,1)S(1)} %get-tuple-element.264), channel_id=1, source_target_pairs={{0,2},{2,0},{4,6},{6,4},{1,3},{3,1},{5,7},{7,5},{8,10},{10,8},{12,... | collective-permute-start | bytes 786440 | tf_op jit(solution)/shard_map/ppermute | solution.py:491
  42.7 4.1 %collective-permute-start.15 = (bf16[2,256,256]{2,1,0:T(8,128)(2,1)S(1)}, bf16[2,256,256]{2,1,0:T(8,128)(2,1)S(1)}, u32[]{:S(2)}, u32[]{:S(2)}) collective-permute-start(bf16[2,256,256]{2,1,0:T(8,128)(2,1)S(1)} %get-tuple-element.273), channel_id=1, source_target_pairs={{0,2},{2,0},{4,6},{6,4},{1,3},{3,1},{5,7},{7,5},{8,10},{10,8},{12,... | collective-permute-start | bytes 786440 | tf_op jit(solution)/shard_map/ppermute | solution.py:491
  65.7 3.0 %collective-permute-start.21 = (bf16[2,256,256]{2,1,0:T(8,128)(2,1)S(1)}, bf16[2,256,256]{2,1,0:T(8,128)(2,1)S(1)}, u32[]{:S(2)}, u32[]{:S(2)}) collective-permute-start(bf16[2,256,256]{2,1,0:T(8,128)(2,1)S(1)} %get-tuple-element.297), channel_id=1, source_target_pairs={{0,2},{2,0},{4,6},{6,4},{1,3},{3,1},{5,7},{7,5},{8,10},{10,8},{12,... | collective-permute-start | bytes 786440 | tf_op jit(solution)/shard_map/ppermute | solution.py:491
  71.4 3.1 %collective-permute-start.27 = (bf16[2,256,256]{2,1,0:T(8,128)(2,1)S(1)}, bf16[2,256,256]{2,1,0:T(8,128)(2,1)S(1)}, u32[]{:S(2)}, u32[]{:S(2)}) collective-permute-start(bf16[2,256,256]{2,1,0:T(8,128)(2,1)S(1)} %get-tuple-element.305), channel_id=1, source_target_pairs={{0,2},{2,0},{4,6},{6,4},{1,3},{3,1},{5,7},{7,5},{8,10},{10,8},{12,... | collective-permute-start | bytes 786440 | tf_op jit(solution)/shard_map/ppermute | solution.py:491
  77.0 3.1 %collective-permute-start.25 = (bf16[2,256,256]{2,1,0:T(8,128)(2,1)S(1)}, bf16[2,256,256]{2,1,0:T(8,128)(2,1)S(1)}, u32[]{:S(2)}, u32[]{:S(2)}) collective-permute-start(bf16[2,256,256]{2,1,0:T(8,128)(2,1)S(1)} %get-tuple-element.309), channel_id=1, source_target_pairs={{0,2},{2,0},{4,6},{6,4},{1,3},{3,1},{5,7},{7,5},{8,10},{10,8},{12,... | collective-permute-start | bytes 786440 | tf_op jit(solution)/shard_map/ppermute | solution.py:491
  82.6 3.4 %collective-permute-start.31 = (bf16[2,256,256]{2,1,0:T(8,128)(2,1)S(1)}, bf16[2,256,256]{2,1,0:T(8,128)(2,1)S(1)}, u32[]{:S(2)}, u32[]{:S(2)}) collective-permute-start(bf16[2,256,256]{2,1,0:T(8,128)(2,1)S(1)} %get-tuple-element.319), channel_id=1, source_target_pairs={{0,2},{2,0},{4,6},{6,4},{1,3},{3,1},{5,7},{7,5},{8,10},{10,8},{12,... | collective-permute-start | bytes 786440 | tf_op jit(solution)/shard_map/ppermute | solution.py:491
  89.0 3.3 %collective-permute-start.29 = (bf16[2,256,256]{2,1,0:T(8,128)(2,1)S(1)}, bf16[2,256,256]{2,1,0:T(8,128)(2,1)S(1)}, u32[]{:S(2)}, u32[]{:S(2)}) collective-permute-start(bf16[2,256,256]{2,1,0:T(8,128)(2,1)S(1)} %get-tuple-element.323), channel_id=1, source_target_pairs={{0,2},{2,0},{4,6},{6,4},{1,3},{3,1},{5,7},{7,5},{8,10},{10,8},{12,... | collective-permute-start | bytes 786440 | tf_op jit(solution)/shard_map/ppermute | solution.py:491
  94.4 3.0 %collective-permute-start.35 = (bf16[2,256,256]{2,1,0:T(8,128)(2,1)S(1)}, bf16[2,256,256]{2,1,0:T(8,128)(2,1)S(1)}, u32[]{:S(2)}, u32[]{:S(2)}) collective-permute-start(bf16[2,256,256]{2,1,0:T(8,128)(2,1)S(1)} %get-tuple-element.337), channel_id=1, source_target_pairs={{0,2},{2,0},{4,6},{6,4},{1,3},{3,1},{5,7},{7,5},{8,10},{10,8},{12,... | collective-permute-start | bytes 786440 | tf_op jit(solution)/shard_map/ppermute | solution.py:491
  100.8 3.1 %collective-permute-start.33 = (bf16[2,256,256]{2,1,0:T(8,128)(2,1)S(1)}, bf16[2,256,256]{2,1,0:T(8,128)(2,1)S(1)}, u32[]{:S(2)}, u32[]{:S(2)}) collective-permute-start(bf16[2,256,256]{2,1,0:T(8,128)(2,1)S(1)} %get-tuple-element.341), channel_id=1, source_target_pairs={{0,2},{2,0},{4,6},{6,4},{1,3},{3,1},{5,7},{7,5},{8,10},{10,8},{12,... | collective-permute-start | bytes 786440 | tf_op jit(solution)/shard_map/ppermute | solution.py:491
  112.7 2.9 %collective-permute-start.37 = (bf16[2,256,256]{2,1,0:T(8,128)(2,1)S(1)}, bf16[2,256,256]{2,1,0:T(8,128)(2,1)S(1)}, u32[]{:S(2)}, u32[]{:S(2)}) collective-permute-start(bf16[2,256,256]{2,1,0:T(8,128)(2,1)S(1)} %get-tuple-element.355), channel_id=1, source_target_pairs={{0,2},{2,0},{4,6},{6,4},{1,3},{3,1},{5,7},{7,5},{8,10},{10,8},{12,... | collective-permute-start | bytes 786440 | tf_op jit(solution)/shard_map/ppermute | solution.py:491
  117.1 3.1 %collective-permute-start.43 = (bf16[2,256,256]{2,1,0:T(8,128)(2,1)S(1)}, bf16[2,256,256]{2,1,0:T(8,128)(2,1)S(1)}, u32[]{:S(2)}, u32[]{:S(2)}) collective-permute-start(bf16[2,256,256]{2,1,0:T(8,128)(2,1)S(1)} %get-tuple-element.368), channel_id=1, source_target_pairs={{0,2},{2,0},{4,6},{6,4},{1,3},{3,1},{5,7},{7,5},{8,10},{10,8},{12,... | collective-permute-start | bytes 786440 | tf_op jit(solution)/shard_map/ppermute | solution.py:491
  122.9 4.1 %collective-permute-start.41 = (bf16[2,256,256]{2,1,0:T(8,128)(2,1)S(1)}, bf16[2,256,256]{2,1,0:T(8,128)(2,1)S(1)}, u32[]{:S(2)}, u32[]{:S(2)}) collective-permute-start(bf16[2,256,256]{2,1,0:T(8,128)(2,1)S(1)} %get-tuple-element.372), channel_id=1, source_target_pairs={{0,2},{2,0},{4,6},{6,4},{1,3},{3,1},{5,7},{7,5},{8,10},{10,8},{12,... | collective-permute-start | bytes 786440 | tf_op jit(solution)/shard_map/ppermute | solution.py:491
  128.6 4.1 %collective-permute-start.47 = (bf16[2,256,256]{2,1,0:T(8,128)(2,1)S(1)}, bf16[2,256,256]{2,1,0:T(8,128)(2,1)S(1)}, u32[]{:S(2)}, u32[]{:S(2)}) collective-permute-start(bf16[2,256,256]{2,1,0:T(8,128)(2,1)S(1)} %get-tuple-element.381), channel_id=1, source_target_pairs={{0,2},{2,0},{4,6},{6,4},{1,3},{3,1},{5,7},{7,5},{8,10},{10,8},{12,... | collective-permute-start | bytes 786440 | tf_op jit(solution)/shard_map/ppermute | solution.py:491
  134.4 4.0 %collective-permute-start.45 = (bf16[2,256,256]{2,1,0:T(8,128)(2,1)S(1)}, bf16[2,256,256]{2,1,0:T(8,128)(2,1)S(1)}, u32[]{:S(2)}, u32[]{:S(2)}) collective-permute-start(bf16[2,256,256]{2,1,0:T(8,128)(2,1)S(1)} %get-tuple-element.385), channel_id=1, source_target_pairs={{0,2},{2,0},{4,6},{6,4},{1,3},{3,1},{5,7},{7,5},{8,10},{10,8},{12,... | collective-permute-start | bytes 786440 | tf_op jit(solution)/shard_map/ppermute | solution.py:491
  146.2 3.2 %collective-permute-start.49 = (bf16[2,256,256]{2,1,0:T(8,128)(2,1)S(1)}, bf16[2,256,256]{2,1,0:T(8,128)(2,1)S(1)}, u32[]{:S(2)}, u32[]{:S(2)}) collective-permute-start(bf16[2,256,256]{2,1,0:T(8,128)(2,1)S(1)} %get-tuple-element.406), channel_id=1, source_target_pairs={{0,2},{2,0},{4,6},{6,4},{1,3},{3,1},{5,7},{7,5},{8,10},{10,8},{12,... | collective-permute-start | bytes 786440 | tf_op jit(solution)/shard_map/ppermute | solution.py:491
  152.2 3.6 %collective-permute-start.57 = (bf16[2,256,256]{2,1,0:T(8,128)(2,1)S(1)}, bf16[2,256,256]{2,1,0:T(8,128)(2,1)S(1)}, u32[]{:S(2)}, u32[]{:S(2)}) collective-permute-start(bf16[2,256,256]{2,1,0:T(8,128)(2,1)S(1)} %get-tuple-element.416), channel_id=1, source_target_pairs={{0,2},{2,0},{4,6},{6,4},{1,3},{3,1},{5,7},{7,5},{8,10},{10,8},{12,... | collective-permute-start | bytes 786440 | tf_op jit(solution)/shard_map/ppermute | solution.py:491
  162.6 3.3 %collective-permute-start.63 = (bf16[2,256,256]{2,1,0:T(8,128)(2,1)S(1)}, bf16[2,256,256]{2,1,0:T(8,128)(2,1)S(1)}, u32[]{:S(2)}, u32[]{:S(2)}) collective-permute-start(bf16[2,256,256]{2,1,0:T(8,128)(2,1)S(1)} %collective-permute-done.58.middle), channel_id=1, source_target_pairs={{0,2},{2,0},{4,6},{6,4},{1,3},{3,1},{5,7},{7,5},{8,10},{10,8},{12,... | collective-permute-start | bytes 786440 | tf_op jit(solution)/shard_map/ppermute | solution.py:491
  169.7 4.8 %collective-permute-done.63.outer_2 = bf16[2,256,256]{2,1,0:T(8,128)(2,1)S(1)} collective-permute-done((bf16[2,256,256]{2,1,0:T(8,128)(2,1)S(1)}, bf16[2,256,256]{2,1,0:T(8,128)(2,1)S(1)}, u32[]{:S(2)}, u32[]{:S(2)}) %collective-permute-start.63) | collective-permute-done | bytes 262176 | tf_op jit(solution)/shard_map/ppermute | solution.py:491
  178.9 5.1 %collective-permute-done.59.outer_2 = bf16[2,256,256]{2,1,0:T(8,128)(2,1)S(1)} collective-permute-done((bf16[2,256,256]{2,1,0:T(8,128)(2,1)S(1)}, bf16[2,256,256]{2,1,0:T(8,128)(2,1)S(1)}, u32[]{:S(2)}, u32[]{:S(2)}) %collective-permute-start.59) | collective-permute-done | bytes 262176 | tf_op jit(solution)/shard_map/ppermute | solution.py:491
  190.3 4.1 %shard_map.172 = f32[1536,768]{1,0:T(8,128)} custom-call(f32[512,768]{1,0:T(8,128)S(1)} %shard_map.123.refs_0_, f32[512,768]{1,0:T(8,128)S(1)} %shard_map.144.refs_1_, f32[512,768]{1,0:T(8,128)S(1)} %shard_map.171.refs_2_, bf16[2,2,256,256]{3,2,1,0:T(8,128)(2,1)S(1)} %shard_map.159.done_ref.refs_0_.refs_3_, ...), custom_call_target="tpu_custom_call" | custom-call | flops 1 | bytes 1 | tf_op jit(solution)/shard_map/pallas_call | solution.py:352
  199.0 6.7 %collective-permute-done.62.refs_1_ = bf16[2,128,768]{2,1,0:T(8,128)(2,1)S(1)} collective-permute-done((bf16[2,128,768]{2,1,0:T(8,128)(2,1)S(1)}, bf16[2,128,768]{2,1,0:T(8,128)(2,1)S(1)}, u32[]{:S(2)}, u32[]{:S(2)}) %collective-permute-start.62) | collective-permute-done | bytes 393248 | tf_op jit(solution)/shard_map/ppermute | solution.py:54
  (234 shorter events, 113.3 us)
Async XLA Ops:
  8.3 18.2 %collective-permute-start.2 = (bf16[2,128,768]{2,1,0:T(8,128)(2,1)S(1)}, bf16[2,128,768]{2,1,0:T(8,128)(2,1)S(1)}, u32[]{:S(2)}, u32[]{:S(2)}) collective-permute-start(bf16[2,128,768]{2,1,0:T(8,128)(2,1)S(1)} %pad_maximum_fusion.refs_0_.refs_1_.refs_4_.refs_7_), channel_id=1, source_target_pairs={{0,1},{1,0},{2,3},{3,2},{4,5},{5,4},{6,7},{7,6},{8,9},{9,8},{10,11... | collective-permute-start | bytes 1179656 | tf_op jit(solution)/shard_map/ppermute | solution.py:54
  17.8 14.1 %collective-permute-start.7 = (bf16[2,128,768]{2,1,0:T(8,128)(2,1)S(1)}, bf16[2,128,768]{2,1,0:T(8,128)(2,1)S(1)}, u32[]{:S(2)}, u32[]{:S(2)}) collective-permute-start(bf16[2,128,768]{2,1,0:T(8,128)(2,1)S(1)} %pad_maximum_fusion.refs_0_.refs_1_.refs_4_.refs_7_), channel_id=1, source_target_pairs={{0,16},{8,24},{16,0},{24,8},{1,17},{9,25},{17,1},{25,9},{2,18},{10... | collective-permute-start | bytes 1179656 | tf_op jit(solution)/shard_map/ppermute | solution.py:54
  19.4 12.5 %collective-permute-start.5 = (bf16[2,256,256]{2,1,0:T(8,128)(2,1)S(1)}, bf16[2,256,256]{2,1,0:T(8,128)(2,1)S(1)}, u32[]{:S(2)}, u32[]{:S(2)}) collective-permute-start(bf16[2,256,256]{2,1,0:T(8,128)(2,1)S(1)} %get-tuple-element.251), channel_id=1, source_target_pairs={{0,2},{2,0},{4,6},{6,4},{1,3},{3,1},{5,7},{7,5},{8,10},{10,8},{12,... | collective-permute-start | bytes 786440 | tf_op jit(solution)/shard_map/ppermute | solution.py:491
  31.9 17.0 %collective-permute-start.11 = (bf16[2,128,768]{2,1,0:T(8,128)(2,1)S(1)}, bf16[2,128,768]{2,1,0:T(8,128)(2,1)S(1)}, u32[]{:S(2)}, u32[]{:S(2)}) collective-permute-start(bf16[2,128,768]{2,1,0:T(8,128)(2,1)S(1)} %collective-permute-done.2.refs_0_.refs_1_), channel_id=1, source_target_pairs={{0,16},{8,24},{16,0},{24,8},{1,17},{9,25},{17,1},{25,9},{2,18},{10... | collective-permute-start | bytes 1179656 | tf_op jit(solution)/shard_map/ppermute | solution.py:54
  35.1 12.4 %collective-permute-start.10 = (bf16[2,256,256]{2,1,0:T(8,128)(2,1)S(1)}, bf16[2,256,256]{2,1,0:T(8,128)(2,1)S(1)}, u32[]{:S(2)}, u32[]{:S(2)}) collective-permute-start(bf16[2,256,256]{2,1,0:T(8,128)(2,1)S(1)} %get-tuple-element.265), channel_id=1, source_target_pairs={{2,4},{4,2},{3,5},{5,3},{10,12},{12,10},{11,13},{13,11},{18,20},{2... | collective-permute-start | bytes 786440 | tf_op jit(solution)/shard_map/ppermute | solution.py:493
  36.5 12.4 %collective-permute-start.9 = (bf16[2,256,256]{2,1,0:T(8,128)(2,1)S(1)}, bf16[2,256,256]{2,1,0:T(8,128)(2,1)S(1)}, u32[]{:S(2)}, u32[]{:S(2)}) collective-permute-start(bf16[2,256,256]{2,1,0:T(8,128)(2,1)S(1)} %get-tuple-element.264), channel_id=1, source_target_pairs={{0,2},{2,0},{4,6},{6,4},{1,3},{3,1},{5,7},{7,5},{8,10},{10,8},{12,... | collective-permute-start | bytes 786440 | tf_op jit(solution)/shard_map/ppermute | solution.py:491
  42.7 11.8 %collective-permute-start.15 = (bf16[2,256,256]{2,1,0:T(8,128)(2,1)S(1)}, bf16[2,256,256]{2,1,0:T(8,128)(2,1)S(1)}, u32[]{:S(2)}, u32[]{:S(2)}) collective-permute-start(bf16[2,256,256]{2,1,0:T(8,128)(2,1)S(1)} %get-tuple-element.273), channel_id=1, source_target_pairs={{0,2},{2,0},{4,6},{6,4},{1,3},{3,1},{5,7},{7,5},{8,10},{10,8},{12,... | collective-permute-start | bytes 786440 | tf_op jit(solution)/shard_map/ppermute | solution.py:491
  77.0 11.9 %collective-permute-start.25 = (bf16[2,256,256]{2,1,0:T(8,128)(2,1)S(1)}, bf16[2,256,256]{2,1,0:T(8,128)(2,1)S(1)}, u32[]{:S(2)}, u32[]{:S(2)}) collective-permute-start(bf16[2,256,256]{2,1,0:T(8,128)(2,1)S(1)} %get-tuple-element.309), channel_id=1, source_target_pairs={{0,2},{2,0},{4,6},{6,4},{1,3},{3,1},{5,7},{7,5},{8,10},{10,8},{12,... | collective-permute-start | bytes 786440 | tf_op jit(solution)/shard_map/ppermute | solution.py:491
  82.6 11.7 %collective-permute-start.31 = (bf16[2,256,256]{2,1,0:T(8,128)(2,1)S(1)}, bf16[2,256,256]{2,1,0:T(8,128)(2,1)S(1)}, u32[]{:S(2)}, u32[]{:S(2)}) collective-permute-start(bf16[2,256,256]{2,1,0:T(8,128)(2,1)S(1)} %get-tuple-element.319), channel_id=1, source_target_pairs={{0,2},{2,0},{4,6},{6,4},{1,3},{3,1},{5,7},{7,5},{8,10},{10,8},{12,... | collective-permute-start | bytes 786440 | tf_op jit(solution)/shard_map/ppermute | solution.py:491
  89.0 11.7 %collective-permute-start.29 = (bf16[2,256,256]{2,1,0:T(8,128)(2,1)S(1)}, bf16[2,256,256]{2,1,0:T(8,128)(2,1)S(1)}, u32[]{:S(2)}, u32[]{:S(2)}) collective-permute-start(bf16[2,256,256]{2,1,0:T(8,128)(2,1)S(1)} %get-tuple-element.323), channel_id=1, source_target_pairs={{0,2},{2,0},{4,6},{6,4},{1,3},{3,1},{5,7},{7,5},{8,10},{10,8},{12,... | collective-permute-start | bytes 786440 | tf_op jit(solution)/shard_map/ppermute | solution.py:491
  94.4 13.0 %collective-permute-start.35 = (bf16[2,256,256]{2,1,0:T(8,128)(2,1)S(1)}, bf16[2,256,256]{2,1,0:T(8,128)(2,1)S(1)}, u32[]{:S(2)}, u32[]{:S(2)}) collective-permute-start(bf16[2,256,256]{2,1,0:T(8,128)(2,1)S(1)} %get-tuple-element.337), channel_id=1, source_target_pairs={{0,2},{2,0},{4,6},{6,4},{1,3},{3,1},{5,7},{7,5},{8,10},{10,8},{12,... | collective-permute-start | bytes 786440 | tf_op jit(solution)/shard_map/ppermute | solution.py:491
  100.8 11.8 %collective-permute-start.33 = (bf16[2,256,256]{2,1,0:T(8,128)(2,1)S(1)}, bf16[2,256,256]{2,1,0:T(8,128)(2,1)S(1)}, u32[]{:S(2)}, u32[]{:S(2)}) collective-permute-start(bf16[2,256,256]{2,1,0:T(8,128)(2,1)S(1)} %get-tuple-element.341), channel_id=1, source_target_pairs={{0,2},{2,0},{4,6},{6,4},{1,3},{3,1},{5,7},{7,5},{8,10},{10,8},{12,... | collective-permute-start | bytes 786440 | tf_op jit(solution)/shard_map/ppermute | solution.py:491
  128.6 13.2 %collective-permute-start.47 = (bf16[2,256,256]{2,1,0:T(8,128)(2,1)S(1)}, bf16[2,256,256]{2,1,0:T(8,128)(2,1)S(1)}, u32[]{:S(2)}, u32[]{:S(2)}) collective-permute-start(bf16[2,256,256]{2,1,0:T(8,128)(2,1)S(1)} %get-tuple-element.381), channel_id=1, source_target_pairs={{0,2},{2,0},{4,6},{6,4},{1,3},{3,1},{5,7},{7,5},{8,10},{10,8},{12,... | collective-permute-start | bytes 786440 | tf_op jit(solution)/shard_map/ppermute | solution.py:491
  134.4 11.7 %collective-permute-start.45 = (bf16[2,256,256]{2,1,0:T(8,128)(2,1)S(1)}, bf16[2,256,256]{2,1,0:T(8,128)(2,1)S(1)}, u32[]{:S(2)}, u32[]{:S(2)}) collective-permute-start(bf16[2,256,256]{2,1,0:T(8,128)(2,1)S(1)} %get-tuple-element.385), channel_id=1, source_target_pairs={{0,2},{2,0},{4,6},{6,4},{1,3},{3,1},{5,7},{7,5},{8,10},{10,8},{12,... | collective-permute-start | bytes 786440 | tf_op jit(solution)/shard_map/ppermute | solution.py:491
  145.0 12.2 %collective-permute-start.51 = (bf16[384,512]{1,0:T(8,128)(2,1)S(1)}, bf16[384,512]{1,0:T(8,128)(2,1)S(1)}, u32[]{:S(2)}, u32[]{:S(2)}) collective-permute-start(bf16[384,512]{1,0:T(8,128)(2,1)S(1)} %shard_map.141), channel_id=1, source_target_pairs={{0,1},{1,0},{2,3},{3,2},{4,5},{5,4},{6,7},{7,6},{8,9},{9,8},{10,11... | collective-permute-start | bytes 1179656 | tf_op jit(solution)/shard_map/ppermute | solution.py:54
  146.2 11.6 %collective-permute-start.49 = (bf16[2,256,256]{2,1,0:T(8,128)(2,1)S(1)}, bf16[2,256,256]{2,1,0:T(8,128)(2,1)S(1)}, u32[]{:S(2)}, u32[]{:S(2)}) collective-permute-start(bf16[2,256,256]{2,1,0:T(8,128)(2,1)S(1)} %get-tuple-element.406), channel_id=1, source_target_pairs={{0,2},{2,0},{4,6},{6,4},{1,3},{3,1},{5,7},{7,5},{8,10},{10,8},{12,... | collective-permute-start | bytes 786440 | tf_op jit(solution)/shard_map/ppermute | solution.py:491
  162.6 11.9 %collective-permute-start.63 = (bf16[2,256,256]{2,1,0:T(8,128)(2,1)S(1)}, bf16[2,256,256]{2,1,0:T(8,128)(2,1)S(1)}, u32[]{:S(2)}, u32[]{:S(2)}) collective-permute-start(bf16[2,256,256]{2,1,0:T(8,128)(2,1)S(1)} %collective-permute-done.58.middle), channel_id=1, source_target_pairs={{0,2},{2,0},{4,6},{6,4},{1,3},{3,1},{5,7},{7,5},{8,10},{10,8},{12,... | collective-permute-start | bytes 786440 | tf_op jit(solution)/shard_map/ppermute | solution.py:491
  169.1 16.8 %collective-permute-start.60 = (bf16[2,128,768]{2,1,0:T(8,128)(2,1)S(1)}, bf16[2,128,768]{2,1,0:T(8,128)(2,1)S(1)}, u32[]{:S(2)}, u32[]{:S(2)}) collective-permute-start(bf16[2,128,768]{2,1,0:T(8,128)(2,1)S(1)} %shard_map.157), channel_id=1, source_target_pairs={{0,16},{8,24},{16,0},{24,8},{1,17},{9,25},{17,1},{25,9},{2,18},{10... | collective-permute-start | bytes 1179656 | tf_op jit(solution)/shard_map/ppermute | solution.py:54
  175.1 12.5 %collective-permute-start.64 = (bf16[2,128,768]{2,1,0:T(8,128)(2,1)S(1)}, bf16[2,128,768]{2,1,0:T(8,128)(2,1)S(1)}, u32[]{:S(2)}, u32[]{:S(2)}) collective-permute-start(bf16[2,128,768]{2,1,0:T(8,128)(2,1)S(1)} %get-tuple-element.460), channel_id=1, source_target_pairs={{0,8},{8,0},{16,24},{24,16},{1,9},{9,1},{17,25},{25,17},{2,10},{10... | collective-permute-start | bytes 1179656 | tf_op jit(solution)/shard_map/ppermute | solution.py:54
  177.7 16.7 %collective-permute-start.68 = (bf16[384,512]{1,0:T(8,128)(2,1)S(1)}, bf16[384,512]{1,0:T(8,128)(2,1)S(1)}, u32[]{:S(2)}, u32[]{:S(2)}) collective-permute-start(bf16[384,512]{1,0:T(8,128)(2,1)S(1)} %shard_map.167), channel_id=1, source_target_pairs={{0,1},{1,0},{2,3},{3,2},{4,5},{5,4},{6,7},{7,6},{8,9},{9,8},{10,11... | collective-permute-start | bytes 1179656 | tf_op jit(solution)/shard_map/ppermute | solution.py:54
  184.6 13.5 %collective-permute-start.67 = (bf16[384,512]{1,0:T(8,128)(2,1)S(1)}, bf16[384,512]{1,0:T(8,128)(2,1)S(1)}, u32[]{:S(2)}, u32[]{:S(2)}) collective-permute-start(bf16[384,512]{1,0:T(8,128)(2,1)S(1)} %shard_map.163), channel_id=1, source_target_pairs={{0,1},{1,0},{2,3},{3,2},{4,5},{5,4},{6,7},{7,6},{8,9},{9,8},{10,11... | collective-permute-start | bytes 1179656 | tf_op jit(solution)/shard_map/ppermute | solution.py:54
  185.8 13.2 %collective-permute-start.66 = (bf16[2,128,768]{2,1,0:T(8,128)(2,1)S(1)}, bf16[2,128,768]{2,1,0:T(8,128)(2,1)S(1)}, u32[]{:S(2)}, u32[]{:S(2)}) collective-permute-start(bf16[2,128,768]{2,1,0:T(8,128)(2,1)S(1)} %get-tuple-element.461), channel_id=1, source_target_pairs={{0,8},{8,0},{16,24},{24,16},{1,9},{9,1},{17,25},{25,17},{2,10},{10... | collective-permute-start | bytes 1179656 | tf_op jit(solution)/shard_map/ppermute | solution.py:54
  186.1 19.7 %collective-permute-start.62 = (bf16[2,128,768]{2,1,0:T(8,128)(2,1)S(1)}, bf16[2,128,768]{2,1,0:T(8,128)(2,1)S(1)}, u32[]{:S(2)}, u32[]{:S(2)}) collective-permute-start(bf16[2,128,768]{2,1,0:T(8,128)(2,1)S(1)} %shard_map.158), channel_id=1, source_target_pairs={{0,1},{1,0},{2,3},{3,2},{4,5},{5,4},{6,7},{7,6},{8,9},{9,8},{10,11... | collective-permute-start | bytes 1179656 | tf_op jit(solution)/shard_map/ppermute | solution.py:54
  187.7 18.0 %collective-permute-start.65 = (bf16[2,128,768]{2,1,0:T(8,128)(2,1)S(1)}, bf16[2,128,768]{2,1,0:T(8,128)(2,1)S(1)}, u32[]{:S(2)}, u32[]{:S(2)}) collective-permute-start(bf16[2,128,768]{2,1,0:T(8,128)(2,1)S(1)} %shard_map.161), channel_id=1, source_target_pairs={{0,16},{8,24},{16,0},{24,8},{1,17},{9,25},{17,1},{25,9},{2,18},{10... | collective-permute-start | bytes 1179656 | tf_op jit(solution)/shard_map/ppermute | solution.py:54
  (54 other events, 477.1 us)
